TPU v7x, 32 devices: a whole 2x2x4 slice. The times are simulated.
32 devices in a mesh: dp: 4 (over y, x), seq: 8 (over z, core).
Axes of the slice: x: 2, y: 2, z: 4, core: 2. Of those that a mesh axis runs over, the one named last changes fastest.
Arguments:
- inputs: bfloat16 [32, 1024, 1024], P('dp', 'seq'), may hold values from -6 to 6
- cotangent: bfloat16 [32, 1024, 1024], P('dp', 'seq'), may hold values from -6 to 6
- lengths: int32 [32], P('dp'), may hold values from 64 to 1024, as said below
- norm_gain: bfloat16 [2, 1024], replicated, may hold values from 0.5 to 1.5
- norm_shift: bfloat16 [2, 1024], replicated, may hold values from -3 to 3
- query_key_value_weight: bfloat16 [1024, 3072], replicated, may hold values from -0.1875 to 0.1875
- output_projection_weight: bfloat16 [1024, 1024], replicated, may hold values from -0.75 to 0.75
- first_feedforward_weight: bfloat16 [1024, 4096], replicated, may hold values from -0.1875 to 0.1875
- second_feedforward_weight: bfloat16 [4096, 1024], replicated, may hold values from -0.09375 to 0.09375
- biases: bfloat16 [8192], replicated, may hold values from -3 to 3
- down_model: float32 [3, 1024, 4], replicated, may hold values from -0.1875 to 0.1875
- down_hidden: float32 [4096, 4], replicated, may hold values from -0.09375 to 0.09375
- query_key_value_upward: float32 [4, 3072], replicated, may hold values from -0.12 to 0.12
- hidden_adapter_upward: float32 [4, 4096], replicated, may hold values from -0.12 to 0.12
- model_adapter_upward: float32 [2, 4, 1024], replicated, may hold values from -0.12 to 0.12
- row_down_model: float32 [3, 1024], replicated, may hold values from 98304 to 1572864
- col_down_model: float32 [3, 4], replicated, may hold values from 98304 to 1572864
- row_down_hidden: float32 [4096], replicated, may hold values from 98304 to 1572864
- col_down_hidden: float32 [4], replicated, may hold values from 98304 to 1572864
- row_up_qkv: float32 [4], replicated, may hold values from 98304 to 1572864
- col_up_qkv: float32 [3072], replicated, may hold values from 98304 to 1572864
- row_up_hidden: float32 [4], replicated, may hold values from 98304 to 1572864
- col_up_hidden: float32 [4096], replicated, may hold values from 98304 to 1572864
- row_up_model: float32 [2, 4], replicated, may hold values from 98304 to 1572864
- col_up_model: float32 [2, 1024], replicated, may hold values from 98304 to 1572864
Outputs:
- output: bfloat16 [32, 1024, 1024], P('dp', 'seq')
- input_grad: bfloat16 [32, 1024, 1024], P('dp', 'seq')
- grad_down_model: float32 [3, 1024, 4], replicated
- grad_down_hidden: float32 [4096, 4], replicated
- grad_up_qkv: float32 [4, 3072], replicated
- grad_up_hidden: float32 [4, 4096], replicated
- grad_up_model: float32 [2, 4, 1024], replicated
- new_down_model: float32 [3, 1024, 4], replicated
- new_down_hidden: float32 [4096, 4], replicated
- new_up_qkv: float32 [4, 3072], replicated
- new_up_hidden: float32 [4, 4096], replicated
- new_up_model: float32 [2, 4, 1024], replicated
- new_row_down_model: float32 [3, 1024], replicated
- new_row_down_hidden: float32 [4096], replicated
- new_row_up_qkv: float32 [4], replicated
- new_row_up_hidden: float32 [4], replicated
- new_row_up_model: float32 [2, 4], replicated
- new_col_down_model: float32 [3, 4], replicated
- new_col_down_hidden: float32 [4], replicated
- new_col_up_qkv: float32 [3072], replicated
- new_col_up_hidden: float32 [4096], replicated
- new_col_up_model: float32 [2, 1024], replicated
Inputs may be any that keep to these rules, and one draw needn't show every extreme that they name: `lengths`: in each aligned block of 8 rows (the rows of one index of dp) one row has length exactly 1024.
All inputs are finite; a program needn't handle non-finite values.
Results may differ from a plain program's by a relative error of at most 0.012.
Values may be sent and summed in bfloat16 or wider, within the bound.
A program may use at most 192 MiB of HBM per device.

v0:
```python
from functools import partial

import jax
import jax.numpy as jnp
from jax import lax
from jax.sharding import PartitionSpec as P

HEADS = 16
HEAD_DIM = 64
STEP = 10


NORM_EPS = 1e-05
ADAPTER_SCALE = 8.0
STAT_EPS = 1e-30
CLIP_LEVEL = 1.0
RATE = 0.3
DECAY_WEIGHT = 0.01
MASKED = -1e30


def as_sent(array):

    def short(part):
        return part.astype(jnp.bfloat16) if part.dtype == jnp.float32 else part

    return jax.tree.map(short, array)


def normalize(values, gain, shift):
    centered = values - jnp.mean(values, axis=-1, keepdims=True)
    spread = jnp.mean(centered * centered, axis=-1, keepdims=True)
    scaled = lax.rsqrt(spread + NORM_EPS)
    unit = centered * scaled
    return (unit * gain + shift, unit, scaled)


def normalize_back(grad, unit, scaled, gain):
    gained = grad * gain
    return scaled * (
        gained
        - jnp.mean(gained, axis=-1, keepdims=True)
        - unit * jnp.mean(gained * unit, axis=-1, keepdims=True)
    )


def matrix_multiply(left, right):
    return jnp.dot(left, right, preferred_element_type=jnp.float32)


def inner_product(left, right):
    return jnp.einsum("tr,tc->rc", left, right, preferred_element_type=jnp.float32)


def compared_with(left, right):
    return jnp.einsum("tc,rc->tr", left, right, preferred_element_type=jnp.float32)


def adapted(source_rows, weight_matrix, bias_vector, down, upward_matrix):
    narrowed_rows = matrix_multiply(source_rows, down).astype(jnp.bfloat16)
    return (
        matrix_multiply(source_rows, weight_matrix)
        + bias_vector
        + ADAPTER_SCALE * matrix_multiply(narrowed_rows, upward_matrix),
        narrowed_rows,
    )


def adapted_back(gradient_lowrank, source_rows, weight_matrix, down, upward_matrix, narrowed_rows):
    gradient_upward = ADAPTER_SCALE * inner_product(narrowed_rows, gradient_lowrank)
    gradient_narrowed = (ADAPTER_SCALE * compared_with(gradient_lowrank, upward_matrix)).astype(
        jnp.bfloat16
    )
    grad_down = inner_product(source_rows, gradient_narrowed)
    grad_source = compared_with(gradient_lowrank, weight_matrix) + compared_with(
        gradient_narrowed, down
    )
    return (grad_source, grad_down, gradient_upward)


def score_block(operand):
    query, keys = operand
    return jnp.einsum("gqe,gke->gqk", query, keys, preferred_element_type=jnp.float32)


def mix_block(operand):
    weights, values = operand
    return jnp.einsum("gqk,gke->gqe", weights, values, preferred_element_type=jnp.float32)


def spread_block(operand):
    weights, queries = operand
    return jnp.einsum("gqk,gqe->gke", weights, queries, preferred_element_type=jnp.float32)


def masked_scores(query, keys, spots, length):
    total = keys.shape[1]
    size = min(512, total)
    reach = jnp.minimum(length, jnp.max(spots) + 1)
    places = jnp.arange(total)
    valid = (places[None, :] <= spots[:, None]) & (places[None, :] < length)
    pieces = []
    for begin in range(0, total, size):
        pieces.append(score_block((query, keys[:, begin : begin + size])))
    scores = jnp.concatenate(pieces, axis=-1) * query.shape[-1] ** (-0.5)
    return (jnp.where(valid[None], scores, MASKED), reach, size)


def attend(query, keys, values, spots, length):
    scores, reach, size = masked_scores(query, keys, spots, length)
    top = jnp.max(scores, axis=-1, keepdims=True)
    weights = jnp.exp(scores - top)
    summed = jnp.sum(weights, axis=-1, keepdims=True)
    probs = (weights / summed).astype(jnp.bfloat16)
    result = jnp.zeros(query.shape, jnp.float32)
    for begin in range(0, keys.shape[1], size):
        operand = (probs[:, :, begin : begin + size], values[:, begin : begin + size])
        result = result + mix_block(operand)
    return (result, (top + jnp.log(summed))[..., 0])


def attend_back(query, keys, values, spots, length, grad_rows, lse):
    scores, reach, size = masked_scores(query, keys, spots, length)
    probs = jnp.exp(scores - lse[..., None])
    pieces = []
    for begin in range(0, keys.shape[1], size):
        pieces.append(score_block((grad_rows, values[:, begin : begin + size])))
    dprob = jnp.concatenate(pieces, axis=-1)
    delta = jnp.sum(probs * dprob, axis=-1, keepdims=True)
    dscore = (probs * (dprob - delta)).astype(jnp.bfloat16)
    probs_low = probs.astype(jnp.bfloat16)
    scale = query.shape[-1] ** (-0.5)
    grad_query = jnp.zeros(query.shape, jnp.float32)
    key_parts = []
    value_parts = []
    for begin in range(0, keys.shape[1], size):
        grad_query = grad_query + mix_block(
            (dscore[:, :, begin : begin + size], keys[:, begin : begin + size])
        )
        key_parts.append(spread_block((dscore[:, :, begin : begin + size], query)))
        value_parts.append(spread_block((probs_low[:, :, begin : begin + size], grad_rows)))
    return (
        grad_query * scale,
        jnp.concatenate(key_parts, axis=1) * scale,
        jnp.concatenate(value_parts, axis=1),
    )


def heads_split(triple):
    return tuple((jnp.transpose(triple[:, index], (1, 0, 2)) for index in range(3)))


def head_forward(skip, item):
    triple, length = item
    spots = jnp.arange(triple.shape[0])
    query, keys, values = heads_split(triple)
    result, lse = attend(query, keys, values, spots, length)
    return (jnp.transpose(result, (1, 0, 2)).astype(jnp.bfloat16), lse)


def head_backward(skip, item):
    triple, grad_rows, lse, length = item
    spots = jnp.arange(triple.shape[0])
    query, keys, values = heads_split(triple)
    grads = attend_back(
        query, keys, values, spots, length, jnp.transpose(grad_rows, (1, 0, 2)), lse
    )
    return jnp.stack(grads, axis=0).transpose(2, 0, 1, 3).astype(jnp.bfloat16)


def factored(grad, weight_matrix, row, col):
    decay = 1.0 - STEP ** (-0.8)
    squares = grad * grad + STAT_EPS
    new_row = decay * row + (1.0 - decay) * jnp.mean(squares, axis=-1)
    new_col = decay * col + (1.0 - decay) * jnp.mean(squares, axis=-2)
    second = (
        new_row[..., :, None] * new_col[..., None, :] / jnp.mean(new_row, axis=-1)[..., None, None]
    )
    unit = grad * lax.rsqrt(second)
    level = jnp.sqrt(jnp.mean(unit * unit, axis=(-2, -1), keepdims=True))
    unit = unit / jnp.maximum(1.0, level / CLIP_LEVEL)
    rate = RATE * jnp.sqrt(jnp.mean(weight_matrix * weight_matrix, axis=(-2, -1), keepdims=True))
    return (weight_matrix - rate * (unit + DECAY_WEIGHT * weight_matrix), new_row, new_col)


def local(
    inputs,
    cotangent,
    lengths,
    norm_gain,
    norm_shift,
    query_key_value_weight,
    output_projection_weight,
    first_feedforward_weight,
    second_feedforward_weight,
    biases,
    down_model,
    down_hidden,
    query_key_value_upward,
    hidden_adapter_upward,
    model_adapter_upward,
    row_down_model,
    col_down_model,
    row_down_hidden,
    col_down_hidden,
    row_up_qkv,
    col_up_qkv,
    row_up_hidden,
    col_up_hidden,
    row_up_model,
    col_up_model,
):
    rows, span, width = inputs.shape
    hidden_width = first_feedforward_weight.shape[1]
    count = rows * span
    spots = lax.axis_index("seq") * span + jnp.arange(span)
    keep = (spots[None, :] < lengths[:, None]).astype(jnp.float32).reshape(count, 1)
    flat = inputs.reshape(count, width).astype(jnp.float32)
    shifts = biases.astype(jnp.float32)
    query_bias = shifts[0:width]
    value_bias = shifts[width : 2 * width]
    projection_bias = shifts[2 * width : 3 * width]
    expand_bias_vector = shifts[3 * width : 3 * width + hidden_width]
    contract_bias_vector = shifts[3 * width + hidden_width : 4 * width + hidden_width]
    query_key_value_bias = jnp.concatenate([query_bias, jnp.zeros_like(query_bias), value_bias])
    gains = norm_gain.astype(jnp.float32)
    offsets = norm_shift.astype(jnp.float32)
    down_low = down_model.astype(jnp.bfloat16)
    hidden_down_low = down_hidden.astype(jnp.bfloat16)
    qkv_up_low = query_key_value_upward.astype(jnp.bfloat16)
    hidden_up_low = hidden_adapter_upward.astype(jnp.bfloat16)
    model_up_low = model_adapter_upward.astype(jnp.bfloat16)
    normalized_rows, unit_first, scaled_first = normalize(flat, gains[0], offsets[0])
    normalized_rows = normalized_rows.astype(jnp.bfloat16)
    mixed_rows, narrow_qkv = adapted(
        normalized_rows, query_key_value_weight, query_key_value_bias, down_low[0], qkv_up_low
    )
    mixed_rows = mixed_rows.astype(jnp.bfloat16).reshape(rows, span, 3, HEADS, HEAD_DIM)
    by_head = lax.all_to_all(mixed_rows, "seq", split_axis=3, concat_axis=1, tiled=True)
    out_heads, lse = lax.map(partial(head_forward, False), (by_head, lengths))
    attended_rows = jax.tree.map(
        lambda part, own: part.astype(own.dtype),
        lax.all_to_all(as_sent(out_heads), "seq", split_axis=1, concat_axis=2, tiled=True),
        out_heads,
    )
    attended_rows = attended_rows.reshape(count, width)
    branch_path, narrow_proj = adapted(
        attended_rows, output_projection_weight, projection_bias, down_low[1], model_up_low[0]
    )
    middle = flat + branch_path
    normed_mid, unit_second, scaled_second = normalize(middle, gains[1], offsets[1])
    normed_mid = normed_mid.astype(jnp.bfloat16)
    before, narrow_expand = adapted(
        normed_mid, first_feedforward_weight, expand_bias_vector, down_low[2], hidden_up_low
    )
    activated, gelu_pull = jax.vjp(lambda value: jax.nn.gelu(value, approximate=True), before)
    activated = activated.astype(jnp.bfloat16)
    branch_out, narrow_contract = adapted(
        activated, second_feedforward_weight, contract_bias_vector, hidden_down_low, model_up_low[1]
    )
    output = (middle + branch_out).astype(jnp.bfloat16).reshape(rows, span, width)
    grad_out = cotangent.reshape(count, width).astype(jnp.float32) * keep
    grad_act, grad_down_contract, grad_up_contract = adapted_back(
        grad_out.astype(jnp.bfloat16),
        activated,
        second_feedforward_weight,
        hidden_down_low,
        model_up_low[1],
        narrow_contract,
    )
    grad_before = gelu_pull(grad_act)[0].astype(jnp.bfloat16)
    grad_norm_mid, grad_down_expand, grad_up_expand = adapted_back(
        grad_before, normed_mid, first_feedforward_weight, down_low[2], hidden_up_low, narrow_expand
    )
    grad_mid = grad_out + normalize_back(grad_norm_mid, unit_second, scaled_second, gains[1])
    grad_att, grad_down_proj, grad_up_proj = adapted_back(
        grad_mid.astype(jnp.bfloat16),
        attended_rows,
        output_projection_weight,
        down_low[1],
        model_up_low[0],
        narrow_proj,
    )
    grad_att = grad_att.astype(jnp.bfloat16).reshape(rows, span, HEADS, HEAD_DIM)
    grad_heads = lax.all_to_all(grad_att, "seq", split_axis=2, concat_axis=1, tiled=True)
    grad_triple = lax.map(partial(head_backward, False), (by_head, grad_heads, lse, lengths))
    grad_mixed = jax.tree.map(
        lambda part, own: part.astype(own.dtype),
        lax.all_to_all(as_sent(grad_triple), "seq", split_axis=1, concat_axis=3, tiled=True),
        grad_triple,
    )
    grad_mixed = grad_mixed.reshape(count, 3 * width)
    grad_normed, grad_down_qkv, grad_up_qkv = adapted_back(
        grad_mixed, normalized_rows, query_key_value_weight, down_low[0], qkv_up_low, narrow_qkv
    )
    input_grad = (
        (grad_mid + normalize_back(grad_normed, unit_first, scaled_first, gains[0]))
        .astype(jnp.bfloat16)
        .reshape(rows, span, width)
    )
    grads = lax.psum(
        (
            jnp.stack([grad_down_qkv, grad_down_proj, grad_down_expand]),
            grad_down_contract,
            grad_up_qkv,
            grad_up_expand,
            jnp.stack([grad_up_proj, grad_up_contract]),
        ),
        ("dp", "seq"),
    )
    grad_dm, grad_dh, grad_uq, grad_uh, grad_um = grads
    new_dm, row_dm, col_dm = factored(grad_dm, down_model, row_down_model, col_down_model)
    new_dh, row_dh, col_dh = factored(grad_dh, down_hidden, row_down_hidden, col_down_hidden)
    new_uq, row_uq, col_uq = factored(grad_uq, query_key_value_upward, row_up_qkv, col_up_qkv)
    new_uh, row_uh, col_uh = factored(grad_uh, hidden_adapter_upward, row_up_hidden, col_up_hidden)
    new_um, row_um, col_um = factored(grad_um, model_adapter_upward, row_up_model, col_up_model)
    return (
        output,
        input_grad,
        grad_dm,
        grad_dh,
        grad_uq,
        grad_uh,
        grad_um,
        new_dm,
        new_dh,
        new_uq,
        new_uh,
        new_um,
        row_dm,
        row_dh,
        row_uq,
        row_uh,
        row_um,
        col_dm,
        col_dh,
        col_uq,
        col_uh,
        col_um,
    )


def solution(mesh):
    placed = (
        P("dp", "seq", None),
        P("dp", "seq", None),
        P("dp"),
        P(),
        P(),
        P(),
        P(),
        P(),
        P(),
        P(),
        P(),
        P(),
        P(),
        P(),
        P(),
        P(),
        P(),
        P(),
        P(),
        P(),
        P(),
        P(),
        P(),
        P(),
        P(),
    )
    return jax.shard_map(
        local,
        mesh=mesh,
        in_specs=placed,
        out_specs=(
            P("dp", "seq", None),
            P("dp", "seq", None),
            P(),
            P(),
            P(),
            P(),
            P(),
            P(),
            P(),
            P(),
            P(),
            P(),
            P(),
            P(),
            P(),
            P(),
            P(),
            P(),
            P(),
            P(),
            P(),
            P(),
        ),
        check_vma=False,
    )
```

profile of v0, /device:TPU:0, one launch (start us, length us, event | category | flops | bytes accessed | tf_op | source)
XLA Modules:
  0.0 1192.6 jit_solution(14692184577894453953)
XLA Ops:
  28.0 16.0 %reshape.399 = bf16[8,128,3,16,64]{4,3,2,1,0:T(8,128)(2,1)} reshape(bf16[1024,3072]{1,0:T(8,128)(2,1)} %add_convert_fusion) | data formatting | bytes 12582912 | tf_op jit(solution)/shard_map/reshape | solution.py:238
  43.9 13.0 %copy.80 = bf16[8,128,3,16,64]{1,0,4,2,3:T(8,128)(2,1)} copy(bf16[8,128,3,16,64]{4,3,2,1,0:T(8,128)(2,1)} %reshape.399) | data formatting | bytes 12582912 | tf_op jit(solution)/shard_map/reshape | solution.py:238
  63.5 139.0 %all-to-all-done = bf16[8,128,3,16,64]{1,0,4,2,3:T(8,128)(2,1)} async-done(((bf16[8,128,3,16,64]{1,0,4,2,3:T(8,128)(2,1)}), bf16[8,128,3,16,64]{1,0,4,2,3:T(8,128)(2,1)}, u32[]{:S(2)}, u32[]{:S(2)}) %all-to-all-start) | async-done | bytes 6291488 | tf_op jit(solution)/shard_map/all_to_all | solution.py:239
  202.5 9.5 copy.81
  212.0 10.3 all_to_all.51
  222.3 97.2 %while.22 = (s32[]{:T(128)}, bf16[8,1024,2,64]{1,3,2,0:T(8,128)(2,1)}, f32[8,2,1024]{2,1,0:T(2,128)}, s32[8]{0:T(128)S(1)}, bf16[8,1024,3,2,64]{1,4,3,2,0:T(8,128)(2,1)}, /*index=5*/s32[]{:T(128)}) while((s32[]{:T(128)}, bf16[8,1024,2,64]{1,3,2,0:T(8,128)(2,1)}, f32[8,2,1024]{2,1,0:T(2,128)}, s32[8]{0:T(128)S(1)}, ...), condition=%wide.region_5.6_spmd, body=%wide.region_2.5_spmd.sunk | while | flops 570686464 | bytes 51185768 | solution.py:240
  319.5 10.9 copy.82
  347.9 14.5 %fusion.195 = f32[1024,4096]{1,0:T(8,128)} fusion(bf16[1024,1024]{1,0:T(8,128)(2,1)S(1)} %fusion.128, bf16[4096,1024]{1,0:T(8,128)(2,1)} %param.37), kind=kOutput, calls=%fused_computation.279 | convolution fusion | flops 8589934592 | bytes 27262976 | tf_op jit(solution)/shard_map/tc,rc->tr/dot_general | solution.py:56
  362.5 29.3 %all-to-all-done.1 = bf16[8,2,65536]{2,1,0:T(2,128)(2,1)} async-done(((bf16[8,2,65536]{2,1,0:T(2,128)(2,1)}), bf16[8,2,65536]{2,1,0:T(2,128)(2,1)}, u32[]{:S(2)}, u32[]{:S(2)}) %all-to-all-start.1) | async-done | bytes 2097184 | tf_op jit(solution)/shard_map/all_to_all | solution.py:243
  399.2 7.9 copy.83
  417.7 11.8 fusion.193
  429.5 15.5 %multiply_convert_fusion.1 = (bf16[1024,4096]{1,0:T(8,128)(2,1)}, f32[1024,4096]{1,0:T(8,128)}) fusion(bf16[1024,4]{0,1:T(4,128)(2,1)S(1)} %convolution_convert_fusion.1, f32[4,4096]{1,0:T(4,128)S(1)} %copy-done.24, f32[1024,4096]{1,0:T(8,128)} %fusion.193, f32[4096]{0:T(1024)S(1)} %slice.157), kind=kOutput, calls=%fused_computation.103 | convolution fusion | flops 83902464 | bytes 42033152 | tf_op jit(solution)/shard_map/dot_general | solution.py:48
  445.0 18.9 %fusion.101 = bf16[1024,4096]{1,0:T(8,128)(2,1)} fusion(f32[1024,4096]{1,0:T(8,128)} %get-tuple-element.173, f32[1024,4096]{1,0:T(8,128)} %fusion.195, bf16[1024,4]{0,1:T(4,128)(2,1)S(1)} %fusion.152, f32[4096,4]{0,1:T(4,128)S(1)} %copy-done.26), kind=kOutput, calls=%fused_computation.102 | convolution fusion | flops 121651200 | bytes 42016768 | tf_op jit(solution)/shard_map/tc,rc->tr/dot_general | solution.py:56
  469.7 11.9 fusion.196
  500.0 49.0 %all-to-all-done.2 = bf16[8,128,16,64]{1,0,3,2:T(8,128)(2,1)S(1)} async-done(((bf16[8,128,16,64]{1,0,3,2:T(8,128)(2,1)}), bf16[8,128,16,64]{1,0,3,2:T(8,128)(2,1)S(1)}, u32[]{:S(2)}, u32[]{:S(2)}) %all-to-all-start.2) | async-done | bytes 2097184 | tf_op jit(solution)/shard_map/all_to_all | solution.py:285
  554.5 201.9 %while.23 = (s32[]{:T(128)}, bf16[8,1024,3,2,64]{1,4,3,2,0:T(8,128)(2,1)}, s32[8]{0:T(128)S(1)}, bf16[8,1024,3,2,64]{1,4,3,2,0:T(8,128)(2,1)}, f32[8,2,1024]{2,1...) while((s32[]{:T(128)}, bf16[8,1024,3,2,64]{1,4,3,2,0:T(8,128)(2,1)}, s32[8]{0:T(128)S(1)}, ...), condition=%wide.region_12.13_spmd, body=%wide.region_10.12_spmd.sunk | while | flops 1379536896 | bytes 83912888 | solution.py:286
  562.2 9.3 multiply_convert_fusion.4
  587.4 9.3 multiply_convert_fusion.4
  612.6 9.3 multiply_convert_fusion.4
  637.9 9.3 multiply_convert_fusion.4
  663.1 9.3 multiply_convert_fusion.4
  688.3 9.3 multiply_convert_fusion.4
  713.5 9.3 multiply_convert_fusion.4
  738.8 9.3 multiply_convert_fusion.4
  756.3 30.6 %copy.86 = bf16[8,1024,3,2,64]{4,3,2,0,1:T(2,128)(2,1)} copy(bf16[8,1024,3,2,64]{1,4,3,2,0:T(8,128)(2,1)} %get-tuple-element.84) | data formatting | bytes 12582912 | tf_op jit(solution)/shard_map/while | solution.py:286
  787.0 13.8 %reshape.402 = bf16[8,2,196608]{2,1,0:T(2,128)(2,1)} reshape(bf16[1024,8,3,2,64]{4,3,2,1,0:T(2,128)(2,1)} %bitcast.298) | data formatting | bytes 12582912
  829.4 13.0 %fusion.194 = f32[1024,1024]{1,0:T(8,128)S(1)} fusion(bf16[1024,4096]{1,0:T(8,128)(2,1)} %get-tuple-element.172, bf16[4096,1024]{1,0:T(8,128)(2,1)} %param.37), kind=kOutput, calls=%fused_computation.278 | convolution fusion | flops 8589934592 | bytes 20971520 | tf_op jit(solution)/shard_map/dot_general | solution.py:48
  845.4 134.7 %all-reduce.7.cloned.1.call-done = (f32[4096,4]{0,1:T(4,128)}, f32[4,4096]{1,0:T(4,128)}) async-done(((f32[4096,4]{0,1:T(4,128)}, f32[4,4096]{1,0:T(4,128)}), (f32[4096,4]{0,1:T(4,128)}, f32[4,4096]{1,0:T(4,128)})) %all-reduce.7.cloned.1.call-update) | async-done | bytes 131088 | tf_op jit(solution)/shard_map/psum | solution.py:301
  990.4 13.4 %reshape.403 = bf16[1024,8,3,2,64]{4,3,2,1,0:T(2,128)(2,1)} reshape(bf16[8,2,196608]{2,1,0:T(2,128)(2,1)} %all-to-all-done.3) | data formatting | bytes 12582912
  1003.9 21.4 %copy.87 = bf16[8,8,128,3,2,64]{2,0,5,4,1,3:T(8,128)(2,1)} copy(bf16[8,8,128,3,2,64]{5,4,3,0,2,1:T(2,128)(2,1)} %bitcast.299) | data formatting | bytes 12582912 | tf_op jit(solution)/shard_map/all_to_all | solution.py:289
  1032.3 9.0 fusion.106
  1052.6 116.6 %all-reduce.5.cloned.1.call-done = (f32[3,1024,4]{1,2,0:T(4,128)}, f32[4,3072]{1,0:T(4,128)}, f32[2,4,1024]{2,1,0:T(4,128)}) async-done(((f32[3,1024,4]{1,2,0:T(4,128)}, f32[4,3072]{1,0:T(4,128)}, f32[2,4,1024]{2,1,0:T(4,128)}), (f32[3,1024,4]{1,2,0:T(4,128)}, f32[4,3072]{1,0:T(4,128)}, f32[2,4,1024]{2,1,0:T(4,128)})) %all-reduce.5.cloned.1.call-update) | async-done | bytes 131088 | tf_op jit(solution)/shard_map/psum | solution.py:301
  (579 shorter events, 385.2 us)
Async XLA Ops:
  7.2 402.0 %copy-start = (bf16[1024,1024]{1,0:T(8,128)(2,1)S(1)}, bf16[1024,1024]{1,0:T(8,128)(2,1)}, u32[]{:S(2)}) copy-start(bf16[1024,1024]{1,0:T(8,128)(2,1)} %param.35) | copy-start | bytes 6291460
  14.3 475.0 %copy-start.34 = (bf16[3,1024,4]{1,2,0:T(4,128)(2,1)}, bf16[3,1024,4]{1,2,0:T(4,128)(2,1)S(1)}, u32[]{:S(2)}) copy-start(bf16[3,1024,4]{1,2,0:T(4,128)(2,1)S(1)} %get-tuple-element.153) | copy-start | bytes 73732
  56.9 145.6 %all-to-all-start = ((bf16[8,128,3,16,64]{1,0,4,2,3:T(8,128)(2,1)}), bf16[8,128,3,16,64]{1,0,4,2,3:T(8,128)(2,1)}, u32[]{:S(2)}, u32[]{:S(2)}) async-start(bf16[8,128,3,16,64]{1,0,4,2,3:T(8,128)(2,1)} %copy.80), calls=%async_computation | async-start | bytes 12582912 | tf_op jit(solution)/shard_map/all_to_all | solution.py:239
  338.0 53.8 %all-to-all-start.1 = ((bf16[8,2,65536]{2,1,0:T(2,128)(2,1)}), bf16[8,2,65536]{2,1,0:T(2,128)(2,1)}, u32[]{:S(2)}, u32[]{:S(2)}) async-start(bf16[8,2,65536]{2,1,0:T(2,128)(2,1)} %reshape.400), calls=%async_computation.1 | async-start | bytes 4194304 | tf_op jit(solution)/shard_map/all_to_all | solution.py:243
  343.5 141.5 %copy-start.35 = (bf16[2,4,1024]{2,1,0:T(4,128)(2,1)}, bf16[2,4,1024]{2,1,0:T(4,128)(2,1)S(1)}, u32[]{:S(2)}) copy-start(bf16[2,4,1024]{2,1,0:T(4,128)(2,1)S(1)} %get-tuple-element.155) | copy-start | bytes 49156
  346.1 98.9 %copy-start.62 = (bf16[1024,4]{0,1:T(4,128)(2,1)}, bf16[1024,4]{0,1:T(4,128)(2,1)S(1)}, u32[]{:S(2)}) copy-start(bf16[1024,4]{0,1:T(4,128)(2,1)S(1)} %fusion.152) | copy-start | bytes 24580
  429.5 15.5 %copy-start.26 = (f32[4096,4]{0,1:T(4,128)S(1)}, f32[4096,4]{0,1:T(4,128)}, u32[]{:S(2)}) copy-start(f32[4096,4]{0,1:T(4,128)} %param.40) | copy-start | bytes 196612
  496.2 52.8 %all-to-all-start.2 = ((bf16[8,128,16,64]{1,0,3,2:T(8,128)(2,1)}), bf16[8,128,16,64]{1,0,3,2:T(8,128)(2,1)S(1)}, u32[]{:S(2)}, u32[]{:S(2)}) async-start(bf16[8,128,16,64]{1,0,3,2:T(8,128)(2,1)} %bitcast.310), calls=%async_computation.2 | async-start | bytes 4194304 | tf_op jit(solution)/shard_map/all_to_all | solution.py:285
  800.8 189.6 %all-to-all-start.3 = ((bf16[8,2,196608]{2,1,0:T(2,128)(2,1)}), bf16[8,2,196608]{2,1,0:T(2,128)(2,1)}, u32[]{:S(2)}, u32[]{:S(2)}) async-start(bf16[8,2,196608]{2,1,0:T(2,128)(2,1)} %reshape.402), calls=%async_computation.3 | async-start | bytes 12582912 | tf_op jit(solution)/shard_map/all_to_all | solution.py:289
  805.8 174.3 %all-reduce.7.cloned.1.call-start = ((), (), s32[]{:S(2)}) async-start(), calls=%async_computation.5 | async-start | bytes 262144 | tf_op jit(solution)/shard_map/psum | solution.py:301
  820.5 348.7 %all-reduce.5.cloned.1.call-start = ((), (), s32[]{:S(2)}) async-start(), calls=%async_computation.4 | async-start | bytes 262144 | tf_op jit(solution)/shard_map/psum | solution.py:301
  842.4 139.7 %copy-start.85 = (f32[4]{0:T(128)S(1)}, f32[4]{0:T(128)}, u32[]{:S(2)}) copy-start(f32[4]{0:T(128)} %param.50) | copy-start | bytes 52
  842.4 139.7 %copy-start.86 = (f32[4]{0:T(128)S(1)}, f32[4]{0:T(128)}, u32[]{:S(2)}) copy-start(f32[4]{0:T(128)} %param.47) | copy-start | bytes 52
  842.4 140.9 %copy-start.70 = (f32[4096]{0:T(1024)S(1)}, f32[4096]{0:T(1024)}, u32[]{:S(2)}) copy-start(f32[4096]{0:T(1024)} %param.46) | copy-start | bytes 49156
  842.4 140.9 %copy-start.71 = (f32[4096]{0:T(1024)S(1)}, f32[4096]{0:T(1024)}, u32[]{:S(2)}) copy-start(f32[4096]{0:T(1024)} %param.51) | copy-start | bytes 49156
  982.7 21.2 %copy-start.76 = (f32[4]{0:T(128)}, f32[4]{0:T(128)S(1)}, u32[]{:S(2)}) copy-start(f32[4]{0:T(128)S(1)} %get-tuple-element.314) | copy-start | bytes 52
  982.7 21.2 %copy-start.77 = (f32[4]{0:T(128)}, f32[4]{0:T(128)S(1)}, u32[]{:S(2)}) copy-start(f32[4]{0:T(128)S(1)} %get-tuple-element.317) | copy-start | bytes 52
  984.0 19.9 %copy-start.45 = (f32[4096]{0:T(1024)}, f32[4096]{0:T(1024)S(1)}, u32[]{:S(2)}) copy-start(f32[4096]{0:T(1024)S(1)} %get-tuple-element.312) | copy-start | bytes 49156
  984.0 19.9 %copy-start.46 = (f32[4096]{0:T(1024)}, f32[4096]{0:T(1024)S(1)}, u32[]{:S(2)}) copy-start(f32[4096]{0:T(1024)S(1)} %get-tuple-element.319) | copy-start | bytes 49156
  1046.5 138.8 %copy-start.1 = (bf16[1024,1024]{1,0:T(8,128)(2,1)S(1)}, bf16[1024,1024]{1,0:T(8,128)(2,1)}, u32[]{:S(2)}) copy-start(bf16[1024,1024]{1,0:T(8,128)(2,1)} %param.35) | copy-start | bytes 6291460
  1046.5 123.5 %copy-start.80 = (f32[2,4]{1,0:T(2,128)S(1)}, f32[2,4]{1,0:T(2,128)}, u32[]{:S(2)}) copy-start(f32[2,4]{1,0:T(2,128)} %param.52) | copy-start | bytes 100
  1046.6 124.6 %copy-start.87 = (f32[4]{0:T(128)S(1)}, f32[4]{0:T(128)}, u32[]{:S(2)}) copy-start(f32[4]{0:T(128)} %param.48) | copy-start | bytes 52
  1046.6 126.8 %copy-start.67 = (f32[3,1024]{1,0:T(4,128)S(1)}, f32[3,1024]{1,0:T(4,128)}, u32[]{:S(2)}) copy-start(f32[3,1024]{1,0:T(4,128)} %param.44) | copy-start | bytes 36868
  1046.6 126.9 %copy-start.74 = (f32[2,1024]{1,0:T(2,128)S(1)}, f32[2,1024]{1,0:T(2,128)}, u32[]{:S(2)}) copy-start(f32[2,1024]{1,0:T(2,128)} %param.53) | copy-start | bytes 24580
  1046.6 127.9 %copy-start.79 = (f32[3,4]{1,0:T(4,128)S(1)}, f32[3,4]{1,0:T(4,128)}, u32[]{:S(2)}) copy-start(f32[3,4]{1,0:T(4,128)} %param.45) | copy-start | bytes 148
  1046.6 128.9 %copy-start.72 = (f32[3072]{0:T(1024)S(1)}, f32[3072]{0:T(1024)}, u32[]{:S(2)}) copy-start(f32[3072]{0:T(1024)} %param.49) | copy-start | bytes 36868
  1046.6 131.1 %copy-start.38 = (f32[2,4,1024]{2,1,0:T(4,128)S(1)}, f32[2,4,1024]{2,1,0:T(4,128)}, u32[]{:S(2)}) copy-start(f32[2,4,1024]{2,1,0:T(4,128)} %param.43) | copy-start | bytes 98308
  1046.6 131.8 %copy-start.33 = (f32[3,1024,4]{1,2,0:T(4,128)S(1)}, f32[3,1024,4]{1,2,0:T(4,128)}, u32[]{:S(2)}) copy-start(f32[3,1024,4]{1,2,0:T(4,128)} %param.39) | copy-start | bytes 147460
  1046.6 134.6 %copy-start.29 = (f32[4096,4]{0,1:T(4,128)S(1)}, f32[4096,4]{0,1:T(4,128)}, u32[]{:S(2)}) copy-start(f32[4096,4]{0,1:T(4,128)} %get-tuple-element.302) | copy-start | bytes 196612
  1046.6 136.6 %copy-start.28 = (f32[4,4096]{1,0:T(4,128)S(1)}, f32[4,4096]{1,0:T(4,128)}, u32[]{:S(2)}) copy-start(f32[4,4096]{1,0:T(4,128)} %get-tuple-element.304) | copy-start | bytes 196612
  1170.2 15.1 %copy-start.75 = (f32[2,4]{1,0:T(2,128)}, f32[2,4]{1,0:T(2,128)S(1)}, u32[]{:S(2)}) copy-start(f32[2,4]{1,0:T(2,128)S(1)} %get-tuple-element.315) | copy-start | bytes 100
  1171.8 13.5 %copy-start.78 = (f32[4]{0:T(128)}, f32[4]{0:T(128)S(1)}, u32[]{:S(2)}) copy-start(f32[4]{0:T(128)S(1)} %get-tuple-element.313) | copy-start | bytes 52
  (80 other events, 479.0 us)
Sparse Core Ops, SparseCore 0:
  820.6 159.3 all-reduce.6
  1046.6 122.5 all-reduce.4
where the time goes:
time: 1210 us; the launch traced here: 1190 us
  waiting for transfers between devices  469 us (39%)
  matrix products  263 us (22%)
  local copies, waits for them, and re-layouts  224 us (19%)
  other arithmetic  195 us (16%)
  between operations  21.7 us (2%)
  starting transfers between devices  20.1 us (2%)
    psum x2, waiting for transfers between devices, local(): lax.psum((jnp.stack([grad_down_qkv, grad_down_proj, grad_down_expand]), g...  251 us
    all_to_all x1, waiting for transfers between devices, local(): lax.all_to_all(mixed_rows, 'seq', split_axis=3, concat_axis=1, tiled=True)  139 us
    sub x8, other arithmetic, attend_back(): dscore = (probs * (dprob - delta)).astype(jnp.bfloat16)  74.6 us
    dot_general x12, matrix products, compared_with(): jnp.einsum('tc,rc->tr', left, right, preferred_element_type=jnp.float32)  74.2 us
    dot_general x12, matrix products, matrix_multiply(): return jnp.dot(left, right, preferred_element_type=jnp.float32)  66.6 us
    unnamed x190, local copies, waits for them, and re-layouts  59 us
    dot_general x32, matrix products, spread_block(): jnp.einsum('gqk,gqe->gke', weights, queries, preferred_element_type=jnp.f...  49.9 us
    all_to_all x1, waiting for transfers between devices, local(): lax.all_to_all(grad_att, 'seq', split_axis=2, concat_axis=1, tiled=True)  49 us
  transfers between devices with their start and end apart: 6, of which 5 were waited for; matrix products, arithmetic and copies ran while one was open for 6% of the time, Pallas kernels for 0%

commit v1 on v0

--- a/solution.py
+++ b/solution.py
@@ -3,6 +3,8 @@
 import jax
 import jax.numpy as jnp
 from jax import lax
+from jax.experimental import pallas as pl
+from jax.experimental.pallas import tpu as pltpu
 from jax.sharding import PartitionSpec as P
 
 HEADS = 16
@@ -183,7 +185,195 @@
     return (weight_matrix - rate * (unit + DECAY_WEIGHT * weight_matrix), new_row, new_col)
 
 
-def local(
+LOG2E = 1.4426950408889634
+TILE = 256
+NT = (((1,), (1,)), ((), ()))
+TN = (((0,), (0,)), ((), ()))
+
+
+def dotf(a, b, dims=(((1,), (0,)), ((), ()))):
+    return lax.dot_general(a, b, dims, preferred_element_type=jnp.float32)
+
+
+def triple(value):
+    high = value.astype(jnp.bfloat16)
+    rest = value - high.astype(jnp.float32)
+    mid = rest.astype(jnp.bfloat16)
+    low = (rest - mid.astype(jnp.float32)).astype(jnp.bfloat16)
+    return high, mid, low
+
+
+def attention_forward_kernel(length_ref, q_ref, k_ref, v_ref, out_ref, lse_ref):
+    total = q_ref.shape[0]
+    wide = q_ref.shape[1]
+    half = wide // 2
+    length = length_ref[0]
+    lane = lax.broadcasted_iota(jnp.int32, (total, wide), 1)
+    spot = lax.broadcasted_iota(jnp.int32, (total, wide), 0)
+    bias = jnp.where(spot < length, 0.0, MASKED).astype(jnp.bfloat16)
+    scale = half ** (-0.5)
+    one = jnp.ones((total, wide), jnp.bfloat16)
+    zero = jnp.zeros((total, wide), jnp.bfloat16)
+    q = q_ref[...] * jnp.asarray(scale, jnp.bfloat16)
+    k = k_ref[...]
+    v = v_ref[...]
+    row = lax.broadcasted_iota(jnp.int32, (TILE, TILE), 0)
+    col = lax.broadcasted_iota(jnp.int32, (TILE, TILE), 1)
+    outs = []
+    lses = []
+    for head in range(2):
+        own = (lane < half) if head == 0 else (lane >= half)
+        spare = half if head == 0 else 0
+        qh = jnp.where(own, q, jnp.where(lane == spare, one, zero))
+        kh = jnp.where(own, k, jnp.where(lane == spare, bias, zero))
+        vh = jnp.where(own, v, one)
+        parts = []
+        lparts = []
+        for begin in range(0, total, TILE):
+            end = begin + TILE
+            scores = dotf(qh[begin:end], kh[:end], NT)
+            diag = jnp.where(col <= row, scores[:, begin:], MASKED)
+            if begin:
+                scores = jnp.concatenate([scores[:, :begin], diag], axis=1)
+            else:
+                scores = diag
+            top = jnp.max(scores, axis=-1, keepdims=True)
+            weights = jnp.exp2((scores - top) * LOG2E).astype(jnp.bfloat16)
+            mixed = dotf(weights, vh[:end])
+            summed = mixed[:, spare : spare + 1]
+            parts.append(mixed * (1.0 / summed))
+            lparts.append(jnp.broadcast_to(top + jnp.log(summed), (TILE, wide)))
+        outs.append(jnp.concatenate(parts, axis=0))
+        lses.append(jnp.concatenate(lparts, axis=0))
+    out_ref[...] = jnp.where(lane < half, outs[0], outs[1]).astype(jnp.bfloat16)
+    lse_ref[0] = jnp.where(lane < half, lses[1], lses[0])
+
+
+def attention_forward(length, mixed):
+    total = mixed.shape[0]
+    width = mixed.shape[1] // 3
+    pairs = width // 128
+
+    def at(offset):
+        return pl.BlockSpec((total, 128), lambda p, s: (0, offset + p))
+
+    return pl.pallas_call(
+        attention_forward_kernel,
+        grid_spec=pltpu.PrefetchScalarGridSpec(
+            num_scalar_prefetch=1,
+            grid=(pairs,),
+            in_specs=[at(0), at(pairs), at(2 * pairs)],
+            out_specs=[
+                at(0),
+                pl.BlockSpec((1, total, 128), lambda p, s: (p, 0, 0)),
+            ],
+        ),
+        out_shape=[
+            jax.ShapeDtypeStruct((total, width), jnp.bfloat16),
+            jax.ShapeDtypeStruct((pairs, total, 128), jnp.float32),
+        ],
+        compiler_params=pltpu.CompilerParams(vmem_limit_bytes=48 * 2**20),
+        name="attention_forward",
+    )(length, mixed, mixed, mixed)
+
+
+def attention_backward_kernel(
+    length_ref, q_ref, k_ref, v_ref, o_ref, g_ref, lse_ref, dq_ref, dk_ref, dv_ref, dq_acc
+):
+    total = q_ref.shape[0]
+    wide = q_ref.shape[1]
+    half = wide // 2
+    length = length_ref[0]
+    lane = lax.broadcasted_iota(jnp.int32, (total, wide), 1)
+    spot = lax.broadcasted_iota(jnp.int32, (total, wide), 0)
+    scale = half ** (-0.5)
+    one = jnp.ones((total, wide), jnp.bfloat16)
+    zero = jnp.zeros((total, wide), jnp.bfloat16)
+    q = q_ref[...] * jnp.asarray(scale, jnp.bfloat16)
+    k = k_ref[...]
+    v = v_ref[...]
+    g = g_ref[...]
+    product = g.astype(jnp.float32) * o_ref[...].astype(jnp.float32)
+    neglse = jnp.where(spot < length, -lse_ref[0], MASKED)
+    row = lax.broadcasted_iota(jnp.int32, (TILE, TILE), 0)
+    col = lax.broadcasted_iota(jnp.int32, (TILE, TILE), 1)
+    l_high, l_mid, l_low = triple(neglse)
+    dks = []
+    dvs = []
+    for head in range(2):
+        own = (lane < half) if head == 0 else (lane >= half)
+        spare = half if head == 0 else 0
+        delta = -jnp.sum(jnp.where(own, product, 0.0), axis=-1, keepdims=True)
+        d_high, d_mid, d_low = triple(jnp.broadcast_to(delta, (total, wide)))
+
+        def extra(a, b, c):
+            return jnp.where(
+                lane == spare, a, jnp.where(lane == spare + 1, b, jnp.where(lane == spare + 2, c, zero))
+            )
+
+        qh = jnp.where(own, q, extra(l_high, l_mid, l_low))
+        kh = jnp.where(own, k, one)
+        gh = jnp.where(own, g, extra(d_high, d_mid, d_low))
+        vh = jnp.where(own, v, one)
+        kz = jnp.where(own, k, zero)
+        dk_parts = []
+        dv_parts = []
+        for begin in range(0, total, TILE):
+            end = begin + TILE
+            scores = dotf(kh[begin:end], qh[begin:], NT)
+            weights = jnp.exp2(scores * LOG2E)
+            diag = jnp.where(row <= col, weights[:, :TILE], 0.0)
+            if end < total:
+                weights = jnp.concatenate([diag, weights[:, TILE:]], axis=1)
+            else:
+                weights = diag
+            dprob = dotf(vh[begin:end], gh[begin:], NT)
+            dscore = (weights * dprob).astype(jnp.bfloat16)
+            dv_parts.append(dotf(weights.astype(jnp.bfloat16), g[begin:]))
+            dk_parts.append(dotf(dscore, q[begin:]))
+            dq_part = dotf(dscore, kz[begin:end], TN)
+            if head == 0 and begin == 0:
+                dq_acc[...] = dq_part
+            else:
+                dq_acc[begin:, :] += dq_part
+        dks.append(jnp.concatenate(dk_parts, axis=0))
+        dvs.append(jnp.concatenate(dv_parts, axis=0))
+    dq_ref[...] = (dq_acc[...] * scale).astype(jnp.bfloat16)
+    dk_ref[...] = jnp.where(lane < half, dks[0], dks[1]).astype(jnp.bfloat16)
+    dv_ref[...] = jnp.where(lane < half, dvs[0], dvs[1]).astype(jnp.bfloat16)
+
+
+def attention_backward(length, mixed, attended, grad, lse):
+    total = mixed.shape[0]
+    width = mixed.shape[1] // 3
+    pairs = width // 128
+
+    def at(offset):
+        return pl.BlockSpec((total, 128), lambda p, s: (0, offset + p))
+
+    return pl.pallas_call(
+        attention_backward_kernel,
+        grid_spec=pltpu.PrefetchScalarGridSpec(
+            num_scalar_prefetch=1,
+            grid=(pairs,),
+            in_specs=[
+                at(0),
+                at(pairs),
+                at(2 * pairs),
+                at(0),
+                at(0),
+                pl.BlockSpec((1, total, 128), lambda p, s: (p, 0, 0)),
+            ],
+            out_specs=[at(0), at(0), at(0)],
+            scratch_shapes=[pltpu.VMEM((total, 128), jnp.float32)],
+        ),
+        out_shape=[jax.ShapeDtypeStruct((total, width), jnp.bfloat16)] * 3,
+        compiler_params=pltpu.CompilerParams(vmem_limit_bytes=48 * 2**20),
+        name="attention_backward",
+    )(length, mixed, mixed, mixed, attended, grad, lse)
+
+
+def local_by_heads(
     inputs,
     cotangent,
     lengths,
@@ -340,6 +530,161 @@
     )
 
 
+def local_by_rows(
+    inputs,
+    cotangent,
+    lengths,
+    norm_gain,
+    norm_shift,
+    query_key_value_weight,
+    output_projection_weight,
+    first_feedforward_weight,
+    second_feedforward_weight,
+    biases,
+    down_model,
+    down_hidden,
+    query_key_value_upward,
+    hidden_adapter_upward,
+    model_adapter_upward,
+    row_down_model,
+    col_down_model,
+    row_down_hidden,
+    col_down_hidden,
+    row_up_qkv,
+    col_up_qkv,
+    row_up_hidden,
+    col_up_hidden,
+    row_up_model,
+    col_up_model,
+):
+    rows, span, width = inputs.shape
+    hidden_width = first_feedforward_weight.shape[1]
+    count = rows * span
+    length = lax.dynamic_slice(lengths, (lax.axis_index("seq"),), (1,))
+    keep = (jnp.arange(count) < length).astype(jnp.float32)[:, None]
+    own_row = lax.all_to_all(inputs, "seq", split_axis=0, concat_axis=0, tiled=True)
+    own_cotangent = lax.all_to_all(cotangent, "seq", split_axis=0, concat_axis=0, tiled=True)
+    flat = own_row.reshape(count, width).astype(jnp.float32)
+    shifts = biases.astype(jnp.float32)
+    query_bias = shifts[0:width]
+    value_bias = shifts[width : 2 * width]
+    projection_bias = shifts[2 * width : 3 * width]
+    expand_bias_vector = shifts[3 * width : 3 * width + hidden_width]
+    contract_bias_vector = shifts[3 * width + hidden_width : 4 * width + hidden_width]
+    query_key_value_bias = jnp.concatenate([query_bias, jnp.zeros_like(query_bias), value_bias])
+    gains = norm_gain.astype(jnp.float32)
+    offsets = norm_shift.astype(jnp.float32)
+    down_low = down_model.astype(jnp.bfloat16)
+    hidden_down_low = down_hidden.astype(jnp.bfloat16)
+    qkv_up_low = query_key_value_upward.astype(jnp.bfloat16)
+    hidden_up_low = hidden_adapter_upward.astype(jnp.bfloat16)
+    model_up_low = model_adapter_upward.astype(jnp.bfloat16)
+    normalized_rows, unit_first, scaled_first = normalize(flat, gains[0], offsets[0])
+    normalized_rows = normalized_rows.astype(jnp.bfloat16)
+    mixed_rows, narrow_qkv = adapted(
+        normalized_rows, query_key_value_weight, query_key_value_bias, down_low[0], qkv_up_low
+    )
+    mixed_rows = mixed_rows.astype(jnp.bfloat16)
+    attended_rows, lse = attention_forward(length, mixed_rows)
+    branch_path, narrow_proj = adapted(
+        attended_rows, output_projection_weight, projection_bias, down_low[1], model_up_low[0]
+    )
+    middle = flat + branch_path
+    normed_mid, unit_second, scaled_second = normalize(middle, gains[1], offsets[1])
+    normed_mid = normed_mid.astype(jnp.bfloat16)
+    before, narrow_expand = adapted(
+        normed_mid, first_feedforward_weight, expand_bias_vector, down_low[2], hidden_up_low
+    )
+    activated, gelu_pull = jax.vjp(lambda value: jax.nn.gelu(value, approximate=True), before)
+    activated = activated.astype(jnp.bfloat16)
+    branch_out, narrow_contract = adapted(
+        activated, second_feedforward_weight, contract_bias_vector, hidden_down_low, model_up_low[1]
+    )
+    output = (middle + branch_out).astype(jnp.bfloat16).reshape(rows, span, width)
+    output = lax.all_to_all(output, "seq", split_axis=0, concat_axis=0, tiled=True)
+    grad_out = own_cotangent.reshape(count, width).astype(jnp.float32) * keep
+    grad_act, grad_down_contract, grad_up_contract = adapted_back(
+        grad_out.astype(jnp.bfloat16),
+        activated,
+        second_feedforward_weight,
+        hidden_down_low,
+        model_up_low[1],
+        narrow_contract,
+    )
+    grad_before = gelu_pull(grad_act)[0].astype(jnp.bfloat16)
+    grad_norm_mid, grad_down_expand, grad_up_expand = adapted_back(
+        grad_before, normed_mid, first_feedforward_weight, down_low[2], hidden_up_low, narrow_expand
+    )
+    grad_mid = grad_out + normalize_back(grad_norm_mid, unit_second, scaled_second, gains[1])
+    grad_att, grad_down_proj, grad_up_proj = adapted_back(
+        grad_mid.astype(jnp.bfloat16),
+        attended_rows,
+        output_projection_weight,
+        down_low[1],
+        model_up_low[0],
+        narrow_proj,
+    )
+    grad_att = grad_att.astype(jnp.bfloat16)
+    grad_mixed = jnp.concatenate(
+        attention_backward(length, mixed_rows, attended_rows, grad_att, lse), axis=1
+    )
+    grad_normed, grad_down_qkv, grad_up_qkv = adapted_back(
+        grad_mixed, normalized_rows, query_key_value_weight, down_low[0], qkv_up_low, narrow_qkv
+    )
+    input_grad = (
+        (grad_mid + normalize_back(grad_normed, unit_first, scaled_first, gains[0]))
+        .astype(jnp.bfloat16)
+        .reshape(rows, span, width)
+    )
+    input_grad = lax.all_to_all(input_grad, "seq", split_axis=0, concat_axis=0, tiled=True)
+    grads = lax.psum(
+        (
+            jnp.stack([grad_down_qkv, grad_down_proj, grad_down_expand]),
+            grad_down_contract,
+            grad_up_qkv,
+            grad_up_expand,
+            jnp.stack([grad_up_proj, grad_up_contract]),
+        ),
+        ("dp", "seq"),
+    )
+    grad_dm, grad_dh, grad_uq, grad_uh, grad_um = grads
+    new_dm, row_dm, col_dm = factored(grad_dm, down_model, row_down_model, col_down_model)
+    new_dh, row_dh, col_dh = factored(grad_dh, down_hidden, row_down_hidden, col_down_hidden)
+    new_uq, row_uq, col_uq = factored(grad_uq, query_key_value_upward, row_up_qkv, col_up_qkv)
+    new_uh, row_uh, col_uh = factored(grad_uh, hidden_adapter_upward, row_up_hidden, col_up_hidden)
+    new_um, row_um, col_um = factored(grad_um, model_adapter_upward, row_up_model, col_up_model)
+    return (
+        output,
+        input_grad,
+        grad_dm,
+        grad_dh,
+        grad_uq,
+        grad_uh,
+        grad_um,
+        new_dm,
+        new_dh,
+        new_uq,
+        new_uh,
+        new_um,
+        row_dm,
+        row_dh,
+        row_uq,
+        row_uh,
+        row_um,
+        col_dm,
+        col_dh,
+        col_uq,
+        col_uh,
+        col_um,
+    )
+
+
+def local(pieces, inputs, *others):
+    if inputs.shape[0] == pieces:
+        return local_by_rows(inputs, *others)
+    return local_by_heads(inputs, *others)
+
+
 def solution(mesh):
     placed = (
         P("dp", "seq", None),
@@ -369,7 +714,7 @@
         P(),
     )
     return jax.shard_map(
-        local,
+        partial(local, mesh.shape["seq"]),
         mesh=mesh,
         in_specs=placed,
         out_specs=(

time: 1210 us -> 670 us (0.55)
  local copies, waits for them, and re-layouts: 224 us -> 17.7 us
  other arithmetic: 195 us -> 45.1 us
  waiting for transfers between devices: 469 us -> 340 us
  matrix products: 263 us -> 148 us
  Pallas kernels: 0 us -> 67.7 us
    all_to_all x4, waiting for transfers between devices: 217 us -> 84.6 us  [the longest x1 43.3 us: local_by_rows(): lax.all_to_all(input_grad, 'seq', split_axis=0, concat_axis=0, tiled=True)]
    dot_general x112 -> x0, matrix products: 107 us -> none  [the longest x32 49.9 us: spread_block(): jnp.einsum('gqk,gqe->gke', weights, queries, preferred_element_type=jnp.f...]
    sub x8 -> x0, other arithmetic: 74.6 us -> none  [attend_back(): dscore = (probs * (dprob - delta)).astype(jnp.bfloat16)]
    pallas_call x0 -> x2, Pallas kernels: none -> 67.7 us  [the longest x1 38 us: attention_backward(): pl.pallas_call(attention_backward_kernel, grid_spec=pltpu.PrefetchScalarG...]
    all_to_all x6 -> x0, local copies, waits for them, and re-layouts: 54.6 us -> none  [the longest x1 21.4 us: local(): lax.all_to_all(as_sent(grad_triple), 'seq', split_axis=1, concat_axis=3,...]
    unnamed x190 -> x155, local copies, waits for them, and re-layouts: 59 us -> 16.3 us
    while x34 -> x0, local copies, waits for them, and re-layouts: 41.6 us -> none  [the longest x1 30.6 us: local(): lax.map(partial(head_backward, False), (by_head, grad_heads, lse, lengths))]
    reshape x2 -> x0, local copies, waits for them, and re-layouts: 29 us -> none  [local(): mixed_rows.astype(jnp.bfloat16).reshape(rows, span, 3, HEADS, HEAD_DIM)]
  transfers between devices with their start and end apart: 6 -> 6, of which waited for: 5 -> 4; matrix products, arithmetic and copies ran while one was open for 6% -> 9% of each run, Pallas kernels for 0% -> 4%
where the time goes in v1:
time: 670 us; the launch traced here: 660 us
  waiting for transfers between devices  340 us (51%)
  matrix products  148 us (22%)
  Pallas kernels  67.7 us (10%)
  other arithmetic  45.1 us (7%)
  between operations  21.5 us (3%)
  starting transfers between devices  20.4 us (3%)
  local copies, waits for them, and re-layouts  17.7 us (3%)
    psum x2, waiting for transfers between devices, local_by_rows(): lax.psum((jnp.stack([grad_down_qkv, grad_down_proj, grad_down_expand]), g...  255 us
    dot_general x12, matrix products, compared_with(): jnp.einsum('tc,rc->tr', left, right, preferred_element_type=jnp.float32)  77.7 us
    dot_general x12, matrix products, matrix_multiply(): return jnp.dot(left, right, preferred_element_type=jnp.float32)  61.6 us
    all_to_all x1, waiting for transfers between devices, local_by_rows(): lax.all_to_all(input_grad, 'seq', split_axis=0, concat_axis=0, tiled=True)  43.3 us
    all_to_all x1, waiting for transfers between devices, local_by_rows(): lax.all_to_all(inputs, 'seq', split_axis=0, concat_axis=0, tiled=True)  41.3 us
    pallas_call x1, Pallas kernels, attention_backward(): pl.pallas_call(attention_backward_kernel, grid_spec=pltpu.PrefetchScalarG...  38 us
    pallas_call x1, Pallas kernels, attention_forward(): pl.pallas_call(attention_forward_kernel, grid_spec=pltpu.PrefetchScalarGr...  29.7 us
    unnamed x155, local copies, waits for them, and re-layouts  16.3 us
  transfers between devices with their start and end apart: 6, of which 4 were waited for; matrix products, arithmetic and copies ran while one was open for 9% of the time, Pallas kernels for 4%

profile of v1, /device:TPU:0, one launch (start us, length us, event | category | flops | bytes accessed | tf_op | source)
XLA Modules:
  0.0 660.5 jit_solution(11895693738395520241)
XLA Ops:
  7.3 6.5 all-to-all-start
  21.6 41.3 %all-to-all-done = bf16[8,128,1024]{2,1,0:T(8,128)(2,1)} async-done(((bf16[8,128,1024]{2,1,0:T(8,128)(2,1)}), bf16[8,128,1024]{2,1,0:T(8,128)(2,1)}, u32[]{:S(2)}, u32[]{:S(2)}) %all-to-all-start) | async-done | bytes 2097184 | tf_op jit(solution)/shard_map/all_to_all | solution.py:565
  62.9 4.4 all-to-all-start.2
  69.3 2.4 fusion.9
  71.8 2.6 fusion.12
  74.3 2.4 fusion.18
  78.1 6.7 %fusion.66 = f32[1024,3072]{1,0:T(8,128)S(1)} fusion(bf16[1024,1024]{1,0:T(8,128)(2,1)S(1)} %fusion.18, bf16[1024,3072]{1,0:T(8,128)(2,1)S(1)} %bitcast.142), kind=kOutput, calls=%fused_computation.168 | convolution fusion | flops 6442450944 | bytes 20971520 | tf_op jit(solution)/shard_map/dot_general | solution.py:50
  84.8 4.6 add_convert_fusion.q_ref.k_ref.v_ref
  89.4 29.7 %attention_forward.1 = (bf16[1024,1024]{1,0:T(8,128)(2,1)S(1)}, f32[8,1024,128]{2,1,0:T(8,128)}) custom-call(s32[1]{0:T(128)} %dynamic_slice.3.length_ref, bf16[1024,3072]{1,0:T(8,128)(2,1)} %add_convert_fusion.q_ref.k_ref.v_ref, bf16[1024,3072]{1,0:T(8,128)(2,1)} %add_convert_fusion.q_ref.k_ref.v_ref, bf16[1024,3072]{1,0:T(8,128)(2,1)} %add_convert_fusion.q_ref.k_ref.v_ref), custom_call_target="tpu_custom_call" | custom-call | tf_op jit(solution)/shard_map/attention_forward/pallas_call | solution.py:260
  120.5 4.3 fusion.67
  127.6 2.9 fusion.65
  135.0 11.6 %fusion.68 = f32[1024,4096]{1,0:T(8,128)} fusion(bf16[1024,1024]{1,0:T(8,128)(2,1)S(1)} %add_convert_fusion.3, bf16[1024,4096]{1,0:T(8,128)(2,1)S(1)} %bitcast.140), kind=kOutput, calls=%fused_computation.170 | convolution fusion | flops 8589934592 | bytes 27262976 | tf_op jit(solution)/shard_map/dot_general | solution.py:50
  146.6 14.5 %multiply_convert_fusion = (bf16[1024,4096]{1,0:T(8,128)(2,1)S(1)}, f32[1024,4096]{1,0:T(8,128)}) fusion(bf16[1024,4]{0,1:T(4,128)(2,1)S(1)} %convolution_convert_fusion.1, f32[4,4096]{1,0:T(4,128)S(1)} %copy-done.17, f32[1024,4096]{1,0:T(8,128)} %fusion.68, f32[4096]{0:T(1024)S(1)} %slice.73), kind=kOutput, calls=%fused_computation.9 | convolution fusion | flops 83902464 | bytes 42033152 | tf_op jit(solution)/shard_map/dot_general | solution.py:50
  165.6 10.4 %fusion.69 = f32[1024,1024]{1,0:T(8,128)} fusion(bf16[1024,4096]{1,0:T(8,128)(2,1)S(1)} %get-tuple-element.89, bf16[4096,1024]{1,0:T(8,128)(2,1)S(1)} %bitcast.138), kind=kOutput, calls=%fused_computation.171 | convolution fusion | flops 8589934592 | bytes 20971520 | tf_op jit(solution)/shard_map/dot_general | solution.py:50
  178.1 15.2 %fusion.70 = f32[1024,4096]{1,0:T(8,128)} fusion(bf16[1024,1024]{1,0:T(8,128)(2,1)S(1)} %fusion.24, bf16[4096,1024]{1,0:T(8,128)(2,1)} %param.33), kind=kOutput, calls=%fused_computation.172 | convolution fusion | flops 8589934592 | bytes 27262976 | tf_op jit(solution)/shard_map/tc,rc->tr/dot_general | solution.py:58
  193.3 18.9 %fusion.6 = bf16[1024,4096]{1,0:T(8,128)(2,1)} fusion(f32[1024,4096]{1,0:T(8,128)} %get-tuple-element.90, f32[1024,4096]{1,0:T(8,128)} %fusion.70, bf16[1024,4]{0,1:T(4,128)(2,1)S(1)} %fusion.27, f32[4096,4]{0,1:T(4,128)S(1)} %copy-done.18), kind=kOutput, calls=%fused_computation.8 | convolution fusion | flops 121651200 | bytes 42016768 | tf_op jit(solution)/shard_map/tc,rc->tr/dot_general | solution.py:58
  212.2 5.8 fusion.28
  219.8 13.0 %fusion.71 = f32[1024,1024]{1,0:T(8,128)S(1)} fusion(bf16[1024,4096]{1,0:T(8,128)(2,1)} %fusion.6, bf16[1024,4096]{1,0:T(8,128)(2,1)} %param.32), kind=kOutput, calls=%fused_computation.173 | convolution fusion | flops 8589934592 | bytes 20971520 | tf_op jit(solution)/shard_map/tc,rc->tr/dot_general | solution.py:58
  234.9 2.8 multiply_add_fusion.1
  239.7 2.4 fusion.51
  244.5 38.0 %attention_backward.1 = (bf16[1024,1024]{1,0:T(8,128)(2,1)S(1)}, bf16[1024,1024]{1,0:T(8,128)(2,1)S(1)}, bf16[1024,1024]{1,0:T(8,128)(2,1)}) custom-call(s32[1]{0:T(128)} %dynamic_slice.3.length_ref, bf16[1024,3072]{1,0:T(8,128)(2,1)} %add_convert_fusion.q_ref.k_ref.v_ref, bf16[1024,3072]{1,0:T(8,128)(2,1)} %add_convert_fusion.q_ref.k_ref.v_ref, ...), custom_call_target="tpu_custom_call" | custom-call | tf_op jit(solution)/shard_map/attention_backward/pallas_call | solution.py:354
  287.6 10.3 %fusion.72 = f32[1024,1024]{1,0:T(8,128)} fusion(bf16[1024,3072]{1,0:T(8,128)(2,1)S(1)} %constant_dynamic-update-slice_fusion, bf16[1024,3072]{1,0:T(8,128)(2,1)} %param.30), kind=kOutput, calls=%fused_computation.174 | convolution fusion | flops 6442450944 | bytes 16777216 | tf_op jit(solution)/shard_map/tc,rc->tr/dot_general | solution.py:58
  298.3 2.3 add_convert_fusion.2
  300.6 5.1 all-to-all-start.1
  307.8 5.4 fusion.55
  314.7 5.8 fusion.23
  320.5 129.1 %all-reduce.7.cloned.1.call-done = (f32[4096,4]{0,1:T(4,128)}, f32[4,4096]{1,0:T(4,128)}) async-done(((f32[4096,4]{0,1:T(4,128)}, f32[4,4096]{1,0:T(4,128)}), (f32[4096,4]{0,1:T(4,128)}, f32[4,4096]{1,0:T(4,128)})) %all-reduce.7.cloned.1.call-update) | async-done | bytes 131088 | tf_op jit(solution)/shard_map/psum | solution.py:640
  452.9 126.2 %all-reduce.5.cloned.1.call-done = (f32[3,1024,4]{1,2,0:T(4,128)}, f32[4,3072]{1,0:T(4,128)}, f32[2,4,1024]{2,1,0:T(4,128)}) async-done(((f32[3,1024,4]{1,2,0:T(4,128)}, f32[4,3072]{1,0:T(4,128)}, f32[2,4,1024]{2,1,0:T(4,128)}), (f32[3,1024,4]{1,2,0:T(4,128)}, f32[4,3072]{1,0:T(4,128)}, f32[2,4,1024]{2,1,0:T(4,128)})) %all-reduce.5.cloned.1.call-update) | async-done | bytes 131088 | tf_op jit(solution)/shard_map/psum | solution.py:640
  590.4 4.3 all-to-all-start.3
  600.5 43.3 %all-to-all-done.3 = bf16[8,128,1024]{2,1,0:T(8,128)(2,1)} async-done(((bf16[8,128,1024]{2,1,0:T(8,128)(2,1)}), bf16[8,128,1024]{2,1,0:T(8,128)(2,1)}, u32[]{:S(2)}, u32[]{:S(2)}) %all-to-all-start.3) | async-done | bytes 2097184 | tf_op jit(solution)/shard_map/all_to_all | solution.py:639
  643.8 3.1 copy.56
  647.0 3.1 copy.57
  (237 shorter events, 60.4 us)
Async XLA Ops:
  7.2 113.3 %copy-start = (bf16[1024,1024]{1,0:T(8,128)(2,1)S(1)}, bf16[1024,1024]{1,0:T(8,128)(2,1)}, u32[]{:S(2)}) copy-start(bf16[1024,1024]{1,0:T(8,128)(2,1)} %param.31) | copy-start | bytes 6291460
  7.3 55.6 %all-to-all-start = ((bf16[8,128,1024]{2,1,0:T(8,128)(2,1)}), bf16[8,128,1024]{2,1,0:T(8,128)(2,1)}, u32[]{:S(2)}, u32[]{:S(2)}) async-start(bf16[8,128,1024]{2,1,0:T(8,128)(2,1)} %param.25), calls=%async_computation | async-start | bytes 4194304 | tf_op jit(solution)/shard_map/all_to_all | solution.py:565
  20.4 107.1 %copy-start.26 = (bf16[2,4,1024]{2,1,0:T(4,128)(2,1)}, bf16[2,4,1024]{2,1,0:T(4,128)(2,1)S(1)}, u32[]{:S(2)}) copy-start(bf16[2,4,1024]{2,1,0:T(4,128)(2,1)S(1)} %get-tuple-element.74) | copy-start | bytes 49156
  62.9 61.8 %all-to-all-start.2 = ((bf16[8,128,1024]{2,1,0:T(8,128)(2,1)}), bf16[8,128,1024]{2,1,0:T(8,128)(2,1)}, u32[]{:S(2)}, u32[]{:S(2)}) async-start(bf16[8,128,1024]{2,1,0:T(8,128)(2,1)} %param.26), calls=%async_computation.2 | async-start | bytes 4194304 | tf_op jit(solution)/shard_map/all_to_all | solution.py:566
  300.6 289.8 %all-to-all-start.1 = ((bf16[8,128,1024]{2,1,0:T(8,128)(2,1)}), bf16[8,128,1024]{2,1,0:T(8,128)(2,1)}, u32[]{:S(2)}, u32[]{:S(2)}) async-start(bf16[8,128,1024]{2,1,0:T(8,128)(2,1)} %bitcast.125), calls=%async_computation.1 | async-start | bytes 4194304 | tf_op jit(solution)/shard_map/all_to_all | solution.py:604
  305.7 143.9 %all-reduce.7.cloned.1.call-start = ((), (), s32[]{:S(2)}) async-start(), calls=%async_computation.5 | async-start | bytes 262144 | tf_op jit(solution)/shard_map/psum | solution.py:640
  313.2 265.9 %all-reduce.5.cloned.1.call-start = ((), (), s32[]{:S(2)}) async-start(), calls=%async_computation.4 | async-start | bytes 262144 | tf_op jit(solution)/shard_map/psum | solution.py:640
  314.6 137.1 %copy-start.63 = (f32[4]{0:T(128)S(1)}, f32[4]{0:T(128)}, u32[]{:S(2)}) copy-start(f32[4]{0:T(128)} %param.46) | copy-start | bytes 52
  314.6 137.1 %copy-start.64 = (f32[4]{0:T(128)S(1)}, f32[4]{0:T(128)}, u32[]{:S(2)}) copy-start(f32[4]{0:T(128)} %param.43) | copy-start | bytes 52
  314.6 265.5 %copy-start.65 = (f32[4]{0:T(128)S(1)}, f32[4]{0:T(128)}, u32[]{:S(2)}) copy-start(f32[4]{0:T(128)} %param.44) | copy-start | bytes 52
  314.6 266.8 %copy-start.50 = (f32[4096]{0:T(1024)S(1)}, f32[4096]{0:T(1024)}, u32[]{:S(2)}) copy-start(f32[4096]{0:T(1024)} %param.42) | copy-start | bytes 49156
  314.6 266.8 %copy-start.51 = (f32[4096]{0:T(1024)S(1)}, f32[4096]{0:T(1024)}, u32[]{:S(2)}) copy-start(f32[4096]{0:T(1024)} %param.47) | copy-start | bytes 49156
  314.6 269.8 %copy-start.60 = (f32[2,4]{1,0:T(2,128)S(1)}, f32[2,4]{1,0:T(2,128)}, u32[]{:S(2)}) copy-start(f32[2,4]{1,0:T(2,128)} %param.48) | copy-start | bytes 100
  314.6 270.0 %copy-start.47 = (f32[3,1024]{1,0:T(4,128)S(1)}, f32[3,1024]{1,0:T(4,128)}, u32[]{:S(2)}) copy-start(f32[3,1024]{1,0:T(4,128)} %param.40) | copy-start | bytes 36868
  314.6 270.1 %copy-start.54 = (f32[2,1024]{1,0:T(2,128)S(1)}, f32[2,1024]{1,0:T(2,128)}, u32[]{:S(2)}) copy-start(f32[2,1024]{1,0:T(2,128)} %param.49) | copy-start | bytes 24580
  314.7 270.1 %copy-start.52 = (f32[3072]{0:T(1024)S(1)}, f32[3072]{0:T(1024)}, u32[]{:S(2)}) copy-start(f32[3072]{0:T(1024)} %param.45) | copy-start | bytes 36868
  320.4 276.4 %copy-start.59 = (f32[3,4]{1,0:T(4,128)S(1)}, f32[3,4]{1,0:T(4,128)}, u32[]{:S(2)}) copy-start(f32[3,4]{1,0:T(4,128)} %param.41) | copy-start | bytes 148
  320.5 276.6 %copy-start.29 = (f32[2,4,1024]{2,1,0:T(4,128)S(1)}, f32[2,4,1024]{2,1,0:T(4,128)}, u32[]{:S(2)}) copy-start(f32[2,4,1024]{2,1,0:T(4,128)} %param.39) | copy-start | bytes 98308
  320.5 276.6 %copy-start.61 = (f32[2]{0:T(128)S(1)}, f32[2]{0:T(128)}, u32[]{:S(2)}) copy-start(f32[2]{0:T(128)} %sqrt_multiply_fusion) | copy-start | bytes 28
  320.5 277.3 %copy-start.25 = (f32[3,1024,4]{1,2,0:T(4,128)S(1)}, f32[3,1024,4]{1,2,0:T(4,128)}, u32[]{:S(2)}) copy-start(f32[3,1024,4]{1,2,0:T(4,128)} %param.35) | copy-start | bytes 147460
  320.5 277.3 %copy-start.62 = (f32[3]{0:T(128)S(1)}, f32[3]{0:T(128)}, u32[]{:S(2)}) copy-start(f32[3]{0:T(128)} %sqrt_multiply_fusion.1) | copy-start | bytes 40
  452.2 194.6 %copy-start.56 = (f32[4]{0:T(128)}, f32[4]{0:T(128)S(1)}, u32[]{:S(2)}) copy-start(f32[4]{0:T(128)S(1)} %get-tuple-element.134) | copy-start | bytes 52
  452.3 194.6 %copy-start.57 = (f32[4]{0:T(128)}, f32[4]{0:T(128)S(1)}, u32[]{:S(2)}) copy-start(f32[4]{0:T(128)S(1)} %get-tuple-element.137) | copy-start | bytes 52
  580.7 66.2 %copy-start.58 = (f32[4]{0:T(128)}, f32[4]{0:T(128)S(1)}, u32[]{:S(2)}) copy-start(f32[4]{0:T(128)S(1)} %get-tuple-element.133) | copy-start | bytes 52
  582.0 64.9 %copy-start.36 = (f32[4096]{0:T(1024)}, f32[4096]{0:T(1024)S(1)}, u32[]{:S(2)}) copy-start(f32[4096]{0:T(1024)S(1)} %get-tuple-element.132) | copy-start | bytes 49156
  582.0 64.9 %copy-start.37 = (f32[4096]{0:T(1024)}, f32[4096]{0:T(1024)S(1)}, u32[]{:S(2)}) copy-start(f32[4096]{0:T(1024)S(1)} %get-tuple-element.139) | copy-start | bytes 49156
  584.6 62.3 %copy-start.55 = (f32[2,4]{1,0:T(2,128)}, f32[2,4]{1,0:T(2,128)S(1)}, u32[]{:S(2)}) copy-start(f32[2,4]{1,0:T(2,128)S(1)} %get-tuple-element.135) | copy-start | bytes 100
  584.7 62.2 %copy-start.34 = (f32[3,1024]{1,0:T(4,128)}, f32[3,1024]{1,0:T(4,128)S(1)}, u32[]{:S(2)}) copy-start(f32[3,1024]{1,0:T(4,128)S(1)} %get-tuple-element.131) | copy-start | bytes 36868
  584.8 62.2 %copy-start.45 = (f32[2,1024]{1,0:T(2,128)}, f32[2,1024]{1,0:T(2,128)S(1)}, u32[]{:S(2)}) copy-start(f32[2,1024]{1,0:T(2,128)S(1)} %multiply_add_fusion.11) | copy-start | bytes 24580
  584.8 62.1 %copy-start.44 = (f32[3072]{0:T(1024)}, f32[3072]{0:T(1024)S(1)}, u32[]{:S(2)}) copy-start(f32[3072]{0:T(1024)S(1)} %multiply_add_fusion.10) | copy-start | bytes 36868
  590.4 53.4 %all-to-all-start.3 = ((bf16[8,128,1024]{2,1,0:T(8,128)(2,1)}), bf16[8,128,1024]{2,1,0:T(8,128)(2,1)}, u32[]{:S(2)}, u32[]{:S(2)}) async-start(bf16[8,128,1024]{2,1,0:T(8,128)(2,1)} %bitcast.128), calls=%async_computation.3 | async-start | bytes 4194304 | tf_op jit(solution)/shard_map/all_to_all | solution.py:639
  596.8 53.2 %copy-start.53 = (f32[3,4]{1,0:T(4,128)}, f32[3,4]{1,0:T(4,128)S(1)}, u32[]{:S(2)}) copy-start(f32[3,4]{1,0:T(4,128)S(1)} %multiply_add_fusion.12) | copy-start | bytes 148
  (47 other events, 556.1 us)
Sparse Core Ops, SparseCore 0:
  313.4 136.2 all-reduce.6
  456.6 122.5 all-reduce.4

commit v2 on v0

--- a/solution.py
+++ b/solution.py
@@ -3,7 +3,10 @@
 import jax
 import jax.numpy as jnp
 from jax import lax
+from jax.experimental import pallas as pl
+from jax.experimental.pallas import tpu as pltpu
 from jax.sharding import PartitionSpec as P
+
 
 HEADS = 16
 HEAD_DIM = 64
@@ -183,7 +186,920 @@
     return (weight_matrix - rate * (unit + DECAY_WEIGHT * weight_matrix), new_row, new_col)
 
 
-def local(
+LOG2E = 1.4426950408889634
+NT = (((1,), (1,)), ((), ()))
+TN = (((0,), (0,)), ((), ()))
+
+
+def dotf(a, b, dims=(((1,), (0,)), ((), ()))):
+    return lax.dot_general(a, b, dims, preferred_element_type=jnp.float32)
+
+
+def triple(value):
+    high = value.astype(jnp.bfloat16)
+    rest = value - high.astype(jnp.float32)
+    mid = rest.astype(jnp.bfloat16)
+    low = (rest - mid.astype(jnp.float32)).astype(jnp.bfloat16)
+    return high, mid, low
+
+
+GELU_A = 0.7978845608028654
+GELU_B = 0.7978845608028654 * 0.044715
+RANK = 4
+
+
+def norm_parts(values):
+    centered = values - jnp.mean(values, axis=-1, keepdims=True)
+    spread = jnp.mean(centered * centered, axis=-1, keepdims=True)
+    scaled = lax.rsqrt(spread + NORM_EPS)
+    return centered * scaled, scaled
+
+
+def norm_back(grad, unit, scaled, gain):
+    gained = grad * gain
+    return scaled * (
+        gained
+        - jnp.mean(gained, axis=-1, keepdims=True)
+        - unit * jnp.mean(gained * unit, axis=-1, keepdims=True)
+    )
+
+
+def low(value):
+    return value.astype(jnp.bfloat16)
+
+
+def wide(value):
+    return value.astype(jnp.float32)
+
+
+def gelu_pair(value):
+    square = value * value
+    half = 0.5 * value
+    bent = jnp.tanh(value * (GELU_A + GELU_B * square))
+    slope = (0.5 + 0.5 * bent) + half * (1.0 - bent * bent) * (GELU_A + 3.0 * GELU_B * square)
+    return half + half * bent, slope
+
+
+def peers_of(axis, size):
+    me = lax.axis_index(axis)
+    return me, [lax.rem(me + shift, size) for shift in range(1, size)]
+
+
+def greet(axes):
+    barrier = pltpu.get_barrier_semaphore()
+    count = 0
+    for axis, size in axes:
+        _, peers = peers_of(axis, size)
+        for peer in peers:
+            pl.semaphore_signal(
+                barrier, inc=1, device_id={axis: peer}, device_id_type=pl.DeviceIdType.MESH
+            )
+        count += len(peers)
+    pl.semaphore_wait(barrier, count)
+
+
+def send(source, target, sent, landed, axis, peer):
+    return pltpu.make_async_remote_copy(
+        src_ref=source,
+        dst_ref=target,
+        send_sem=sent,
+        recv_sem=landed,
+        device_id={axis: peer},
+        device_id_type=pl.DeviceIdType.MESH,
+    )
+
+
+def sum_everywhere(
+    splits, copies, part_ref, total_ref, seq_in, dp_in, own, s_sent, s_land, d_sent, d_land, g_sent, g_land
+):
+    size = part_ref.shape[1] // splits
+    me, peers = peers_of("seq", splits)
+    mine, others = peers_of("dp", copies)
+
+    def columns(index):
+        return pl.ds(pl.multiple_of(index * size, size), size)
+
+    first = []
+    for shift, peer in enumerate(peers):
+        copy = send(part_ref.at[:, columns(peer)], seq_in.at[me], s_sent.at[shift], s_land.at[me], "seq", peer)
+        copy.start()
+        first.append(copy)
+    seq_in[me] = part_ref[:, columns(me)]
+    for peer in peers:
+        send(part_ref.at[:, columns(me)], seq_in.at[peer], s_sent.at[0], s_land.at[peer], "seq", peer).wait_recv()
+    summed = seq_in[0]
+    for index in range(1, splits):
+        summed = summed + seq_in[index]
+    own[...] = summed
+    second = []
+    for shift, peer in enumerate(others):
+        copy = send(own, dp_in.at[mine], d_sent.at[shift], d_land.at[mine], "dp", peer)
+        copy.start()
+        second.append(copy)
+    dp_in[mine] = summed
+    for peer in others:
+        send(own, dp_in.at[peer], d_sent.at[0], d_land.at[peer], "dp", peer).wait_recv()
+    summed = dp_in[0]
+    for index in range(1, copies):
+        summed = summed + dp_in[index]
+    total_ref[:, columns(me)] = summed
+    third = []
+    for shift, peer in enumerate(peers):
+        copy = send(
+            total_ref.at[:, columns(me)], total_ref.at[:, columns(me)], g_sent.at[shift], g_land.at[me], "seq", peer
+        )
+        copy.start()
+        third.append(copy)
+    for peer in peers:
+        part = total_ref.at[:, columns(peer)]
+        send(part, part, g_sent.at[0], g_land.at[peer], "seq", peer).wait_recv()
+    for copy in first + second + third:
+        copy.wait_send()
+
+
+def sum_scratch(splits, copies, width):
+    size = width // splits
+    dma = pltpu.SemaphoreType.DMA
+    return [
+        pltpu.VMEM((splits, 8, size), jnp.float32),
+        pltpu.VMEM((copies, 8, size), jnp.float32),
+        pltpu.VMEM((8, size), jnp.float32),
+        dma((splits,)),
+        dma((splits,)),
+        dma((copies,)),
+        dma((copies,)),
+        dma((splits,)),
+        dma((splits,)),
+    ]
+
+
+def across(column):
+    count = column.shape[0]
+    diagonal = lax.broadcasted_iota(jnp.int32, (count, count), 0) == lax.broadcasted_iota(
+        jnp.int32, (count, count), 1
+    )
+    return jnp.sum(jnp.where(diagonal, jnp.broadcast_to(column, (count, count)), 0.0), axis=0, keepdims=True)
+
+
+def upright(line):
+    count = line.shape[1]
+    diagonal = lax.broadcasted_iota(jnp.int32, (count, count), 0) == lax.broadcasted_iota(
+        jnp.int32, (count, count), 1
+    )
+    return jnp.sum(jnp.where(diagonal, jnp.broadcast_to(line, (count, count)), 0.0), axis=1, keepdims=True)
+
+
+def factored_step(grad, weight, short_line, long_line, rows_long):
+    decay = 1.0 - STEP ** (-0.8)
+    squares = grad * grad + STAT_EPS
+    new_short = decay * upright(short_line) + (1.0 - decay) * jnp.mean(squares, axis=1, keepdims=True)
+    new_long = decay * long_line + (1.0 - decay) * jnp.mean(squares, axis=0, keepdims=True)
+    if rows_long:
+        middle = jnp.mean(new_long, axis=1, keepdims=True)
+    else:
+        middle = jnp.mean(new_short, axis=0, keepdims=True)
+    unit = grad * lax.rsqrt(new_short * new_long / middle)
+    entries = grad.shape[0] * grad.shape[1]
+
+    def mean_square(value):
+        return jnp.sum(jnp.sum(value * value, axis=1, keepdims=True), axis=0, keepdims=True) / entries
+
+    level = jnp.sqrt(mean_square(unit))
+    unit = unit / jnp.maximum(1.0, level / CLIP_LEVEL)
+    rate = RATE * jnp.sqrt(mean_square(weight))
+    return weight - rate * (unit + DECAY_WEIGHT * weight), across(new_short), new_long
+
+
+def update_kernel(
+    total_ref, output_in, grad_in, dm, dh, uq, uh, um, row_dm, col_dm, row_dh, col_dh, row_uq, col_uq, row_uh, col_uh, row_um, col_um,
+    output_out, grad_out, g_dm, g_dh, g_uq, g_uh, g_um, n_dm, n_dh, n_uq, n_uh, n_um,
+    r_dm, r_dh, r_uq, r_uh, r_um, c_dm, c_dh, c_uq, c_uh, c_um, held_out, held_grad, sems,
+):
+    moves = [
+        pltpu.make_async_copy(output_in, held_out, sems.at[0]),
+        pltpu.make_async_copy(grad_in, held_grad, sems.at[1]),
+    ]
+    for move in moves:
+        move.start()
+    moves = [
+        (moves[0], pltpu.make_async_copy(held_out, output_out, sems.at[0])),
+        (moves[1], pltpu.make_async_copy(held_grad, grad_out, sems.at[1])),
+    ]
+    for move, onward in moves:
+        move.wait()
+        onward.start()
+    width = dm.shape[2]
+    hidden = dh.shape[1]
+    for index in range(3):
+        grad = total_ref[0:RANK, index * width : (index + 1) * width]
+        g_dm[index] = grad
+        n_dm[index], c_dm[index : index + 1, :], r_dm[index : index + 1, :] = factored_step(
+            grad, dm[index], col_dm[index : index + 1, :], row_dm[index : index + 1, :], True
+        )
+    grad = total_ref[0:RANK, 3 * width : 6 * width]
+    g_uq[...] = grad
+    n_uq[...], r_uq[...], c_uq[...] = factored_step(grad, uq[...], row_uq[...], col_uq[...], False)
+    for index in range(2):
+        grad = total_ref[0:RANK, (6 + index) * width : (7 + index) * width]
+        g_um[index] = grad
+        n_um[index], r_um[index : index + 1, :], c_um[index : index + 1, :] = factored_step(
+            grad, um[index], row_um[index : index + 1, :], col_um[index : index + 1, :], False
+        )
+    grad = total_ref[RANK : 2 * RANK, 0:hidden]
+    g_dh[...] = grad
+    n_dh[...], c_dh[...], r_dh[...] = factored_step(grad, dh[...], col_dh[...], row_dh[...], True)
+    grad = total_ref[RANK : 2 * RANK, hidden : 2 * hidden]
+    g_uh[...] = grad
+    n_uh[...], r_uh[...], c_uh[...] = factored_step(grad, uh[...], row_uh[...], col_uh[...], False)
+    for _, onward in moves:
+        onward.wait()
+
+
+def update(total, output, input_grad, adapters, row_dm, col_dm, row_dh, col_dh, row_uq, col_uq, row_uh, col_uh, row_um, col_um):
+    flip = lambda array: jnp.swapaxes(array, -1, -2)
+    line = lambda array: array.reshape(1, -1)
+    given = [
+        row_dm, col_dm, line(row_dh), line(col_dh), line(row_uq), line(col_uq), line(row_uh), line(col_uh), row_um, col_um,
+    ]
+    stats = given[0::2] + given[1::2]
+    anyspace = pl.BlockSpec(memory_space=pl.ANY)
+    vmem = pl.BlockSpec(memory_space=pltpu.VMEM)
+    results = pl.pallas_call(
+        update_kernel,
+        out_shape=[jax.ShapeDtypeStruct(a.shape, a.dtype) for a in [output, input_grad] + adapters + adapters + stats],
+        in_specs=[vmem, anyspace, anyspace] + [vmem] * 15,
+        out_specs=[anyspace, anyspace] + [vmem] * 20,
+        scratch_shapes=[
+            pltpu.VMEM(output.shape, output.dtype),
+            pltpu.VMEM(output.shape, output.dtype),
+            pltpu.SemaphoreType.DMA((2,)),
+        ],
+        compiler_params=pltpu.CompilerParams(vmem_limit_bytes=24 * 2**20),
+        name="factored_update",
+    )(total, output, input_grad, *adapters, *given)
+    results = list(results)
+    for index in (2, 3, 7, 8):
+        results[index] = flip(results[index])
+    olds = (row_dm, row_dh, row_uq, row_uh, row_um, col_dm, col_dh, col_uq, col_uh, col_um)
+    for index, old in zip(range(12, 22), olds):
+        results[index] = results[index].reshape(old.shape)
+    return tuple(results)
+
+
+TILE = 256
+GROUP = 4
+LANES = 128
+
+
+def peer_order(me, splits, far_first):
+    half = splits // 2
+    side, place = me // half, lax.rem(me, half)
+    far = [(1 - side) * half + lax.rem(place + shift, half) for shift in range(half)]
+    near = [side * half + lax.rem(place + shift, half) for shift in range(1, half)]
+    return far + near if far_first else near + far
+
+
+def fill_adapters(dm_ref, dh_ref, uq_ref, uh_ref, um_ref, aq, ap, a1, a2, bq, bp, b2, b1):
+    for index, ref in enumerate((aq, ap, a1)):
+        ref[...] = low(dm_ref[index])
+    a2[...] = low(dh_ref[...])
+    for ref, value in ((bq, uq_ref[...]), (bp, um_ref[0]), (b2, um_ref[1]), (b1, uh_ref[...])):
+        ref[...] = low(ADAPTER_SCALE * wide(low(value)))
+
+
+def adapter_scratch(width, hidden):
+    sizes = [width, width, width, hidden, 3 * width, width, width, hidden]
+    return [pltpu.VMEM((RANK, size), jnp.bfloat16) for size in sizes]
+
+
+def forward_kernel(
+    splits, solo,
+    lengths_ref, inputs, cotangent, wqkv_hbm, wo_hbm, w1_hbm, w2_hbm,
+    bias_ref, gain_ref, shift_ref, dm_ref, dh_ref, uq_ref, uh_ref, um_ref,
+    x_out, cot_out, out_out, qx_out, kx_out, vx_out, att_out, mid_out, nmid_out, act_out, slope_out, narrow_out,
+    xr, wqkv, wo, w1, w2, kx, vx, qs, qb, att, mid, nmid, act, slope, outs, narrow,
+    aq, ap, a1, a2, bq, bp, b2, b1,
+    w_sem, x_sent, x_land, c_sent, c_land, o_sem, kv_sem, own_sem,
+):
+    me = 0 if solo else lax.axis_index("seq")
+    span, width = xr.shape[1], xr.shape[2]
+    total = splits * span
+    hidden = w1.shape[1]
+    blocks = TILE // span
+    heads = kx.shape[0]
+    half = LANES // 2
+    length = lengths_ref[me]
+    loads = [
+        pltpu.make_async_copy(source, target, w_sem.at[index])
+        for index, (source, target) in enumerate(((wqkv_hbm, wqkv), (wo_hbm, wo), (w1_hbm, w1), (w2_hbm, w2)))
+    ]
+    own_x = pltpu.make_async_copy(inputs.at[me], xr.at[me], own_sem.at[0])
+    own_c = pltpu.make_async_copy(cotangent.at[me], cot_out.at[me], own_sem.at[1])
+    save_x = pltpu.make_async_copy(xr, x_out, own_sem.at[2])
+    if not solo:
+        greet((("seq", splits),))
+        own_x.start()
+    else:
+        all_x = pltpu.make_async_copy(inputs, xr, own_sem.at[0])
+        all_x.start()
+    loads[0].start()
+
+    def x_copy(peer, slot):
+        return send(inputs.at[peer], xr.at[me], x_sent.at[slot], x_land.at[me], "seq", peer)
+
+    def c_copy(peer, slot):
+        return send(cotangent.at[peer], cot_out.at[me], c_sent.at[slot], c_land.at[me], "seq", peer)
+
+    if not solo:
+        pair = me // 2
+        outward = jnp.logical_or(pair == 0, pair == splits // 2 - 2)
+
+        @pl.when(outward)
+        def _():
+            for slot, peer in enumerate(peer_order(me, splits, True)):
+                x_copy(peer, slot).start()
+
+        @pl.when(jnp.logical_not(outward))
+        def _():
+            for slot, peer in enumerate(peer_order(me, splits, False)):
+                x_copy(peer, slot).start()
+
+    for load in loads[1:]:
+        load.start()
+    fill_adapters(dm_ref, dh_ref, uq_ref, uh_ref, um_ref, aq, ap, a1, a2, bq, bp, b2, b1)
+    if solo:
+        all_x.wait()
+    else:
+        own_x.wait()
+
+    lane = lax.broadcasted_iota(jnp.int32, (TILE, LANES), 1)
+    row = lax.broadcasted_iota(jnp.int32, (TILE, TILE), 0)
+    col = lax.broadcasted_iota(jnp.int32, (TILE, TILE), 1)
+    causal = col <= row
+    zero = jnp.zeros((TILE, LANES), jnp.bfloat16)
+    one = jnp.ones((TILE, LANES), jnp.bfloat16)
+    scale = jnp.asarray(half ** (-0.5), jnp.bfloat16)
+    owns = (lane < half, lane >= half)
+    spares = (half, 0)
+
+    def bias(start, size):
+        return wide(bias_ref[0:1, start : start + size])
+
+    def saves(tile):
+        rows = pl.ds(tile * TILE, TILE)
+        return [
+            pltpu.make_async_copy(source, target, o_sem.at[index])
+            for index, (source, target) in enumerate(
+                (
+                    (qb, qx_out.at[:, rows, :]),
+                    (att, att_out.at[:, rows, :]),
+                    (mid, mid_out.at[rows, :]),
+                    (nmid, nmid_out.at[rows, :]),
+                    (act, act_out.at[rows, :]),
+                    (slope, slope_out.at[rows, :]),
+                    (outs, out_out.at[rows, :]),
+                    (narrow, narrow_out.at[rows, :]),
+                )
+            )
+        ]
+
+    def kv_saves(tile):
+        rows = pl.ds(tile * TILE, TILE)
+        return [
+            pltpu.make_async_copy(kx.at[:, rows, :], kx_out.at[:, rows, :], kv_sem.at[2 * tile]),
+            pltpu.make_async_copy(vx.at[:, rows, :], vx_out.at[:, rows, :], kv_sem.at[2 * tile + 1]),
+        ]
+
+    tiles = total // TILE
+    for tile in range(tiles):
+        begin, end = tile * TILE, (tile + 1) * TILE
+        for block in range(tile * blocks, (tile + 1) * blocks):
+            if solo:
+                continue
+
+            @pl.when(me != block)
+            def _():
+                send(inputs.at[block], xr.at[block], x_sent.at[0], x_land.at[block], "seq", block).wait_recv()
+
+        if tile == tiles - 1 and not solo:
+            save_x.start()
+            own_c.start()
+            for slot, peer in enumerate(peer_order(me, splits, True)):
+                c_copy(peer, slot).start()
+        if tile == 0:
+            loads[0].wait()
+        else:
+            saves(tile - 1)[7].wait()
+        x = wide(xr[tile * blocks : (tile + 1) * blocks].reshape(TILE, width))
+        unit, _ = norm_parts(x)
+        normed = low(unit * wide(gain_ref[0:1, :]) + wide(shift_ref[0:1, :]))
+        narrow_q = low(dotf(normed, aq[...], NT))
+        narrow[:, 0:RANK] = narrow_q
+        spot = begin + lax.broadcasted_iota(jnp.int32, (TILE, LANES), 0)
+        valid = spot < length
+        limit = jnp.where(valid, 0.0, MASKED).astype(jnp.bfloat16)
+        size = 512
+        for part in range(3):
+            for start in range(0, width, size):
+                column = part * width + start
+                value = dotf(normed, wqkv[:, column : column + size]) + dotf(narrow_q, bq[:, column : column + size])
+                if part == 0:
+                    value = value + bias(start, size)
+                if part == 2:
+                    value = value + bias(width + start, size)
+                value = low(value)
+                for index in range(size // LANES):
+                    piece = value[:, index * LANES : (index + 1) * LANES]
+                    for parity in range(2):
+                        head = 2 * (start // LANES + index) + parity
+                        own, spare = owns[parity], spares[parity]
+                        if part == 0:
+                            qs[head] = jnp.where(own, piece * scale, jnp.where(lane == spare + 3, one, zero))
+                        elif part == 1:
+                            extra = jnp.where(lane == spare + 3, limit, jnp.where(lane < spare + 3, one, zero))
+                            kx[head, begin:end, :] = jnp.where(own, piece, extra)
+                        else:
+                            vx[head, begin:end, :] = jnp.where(own, piece, one)
+        for save in kv_saves(tile):
+            save.start()
+        if tile:
+            for save in saves(tile - 1)[0:2]:
+                save.wait()
+
+        def attend(index, carry):
+            def scores(unit):
+                head = index * GROUP + unit
+                return dotf(qs[head], kx[head, 0:end, :], NT)
+
+            def mix(unit, value):
+                head = index * GROUP + unit
+                last = jnp.where(causal, value[:, begin:], MASKED)
+                value = jnp.concatenate([value[:, :begin], last], axis=1) if begin else last
+                top = jnp.max(value, axis=-1, keepdims=True)
+                weights = low(jnp.exp2((value - top) * LOG2E))
+                mixed = dotf(weights, vx[head, 0:end, :])
+                spare, own = spares[unit % 2], owns[unit % 2]
+                summed = mixed[:, spare : spare + 1]
+                back = jnp.where(valid, -(top + jnp.log(summed)), MASKED)
+                high, middle, rest = triple(back)
+                extra = jnp.where(
+                    lane == spare, high, jnp.where(lane == spare + 1, middle, jnp.where(lane == spare + 2, rest, zero))
+                )
+                qb[head] = jnp.where(own, qs[head], extra)
+                return mixed * (1.0 / summed)
+
+            ahead = scores(0)
+            results = []
+            for unit in range(GROUP):
+                value = ahead
+                if unit + 1 < GROUP:
+                    ahead = scores(unit + 1)
+                results.append(mix(unit, value))
+            for unit in range(0, GROUP, 2):
+                att[index * (GROUP // 2) + unit // 2] = low(jnp.where(owns[0], results[unit], results[unit + 1]))
+            return carry
+
+        lax.fori_loop(0, heads // GROUP, attend, 0)
+        for save in saves(tile)[0:2]:
+            save.start()
+        if tile == 0:
+            for load in loads[1:]:
+                load.wait()
+        else:
+            for save in saves(tile - 1)[2:7]:
+                save.wait()
+        attended = jnp.concatenate([att[index] for index in range(heads // 2)], axis=1)
+        narrow_p = low(dotf(attended, ap[...], NT))
+        middle = (
+            wide(xr[tile * blocks : (tile + 1) * blocks].reshape(TILE, width))
+            + dotf(attended, wo[...])
+            + bias(2 * width, width)
+            + dotf(narrow_p, bp[...])
+        )
+        mid[...] = middle
+        unit, _ = norm_parts(middle)
+        normed = low(unit * wide(gain_ref[1:2, :]) + wide(shift_ref[1:2, :]))
+        nmid[...] = normed
+        narrow_1 = low(dotf(normed, a1[...], NT))
+        size = 256
+
+        def expand(start):
+            return (
+                dotf(normed, w1[:, start : start + size])
+                + bias(3 * width + start, size)
+                + dotf(narrow_1, b1[:, start : start + size])
+            )
+
+        result = middle + bias(3 * width + hidden, width)
+        narrow_2 = jnp.zeros((TILE, RANK), jnp.float32)
+        ahead = expand(0)
+        for start in range(0, hidden, size):
+            stop = start + size
+            before = ahead
+            if stop < hidden:
+                ahead = expand(stop)
+            active, bend = gelu_pair(before)
+            active = low(active)
+            act[:, start:stop] = active
+            slope[:, start:stop] = low(bend)
+            result = result + dotf(active, w2[start:stop, :])
+            narrow_2 = narrow_2 + dotf(active, a2[:, start:stop], NT)
+        narrow_2 = low(narrow_2)
+        outs[...] = low(result + dotf(narrow_2, b2[...]))
+        narrow[:, RANK : 2 * RANK] = narrow_p
+        narrow[:, 2 * RANK : 3 * RANK] = narrow_1
+        narrow[:, 3 * RANK : 4 * RANK] = narrow_2
+        for save in saves(tile)[2:8]:
+            save.start()
+
+    for save in saves(tiles - 1):
+        save.wait()
+    for tile in range(tiles):
+        for save in kv_saves(tile):
+            save.wait()
+    if solo:
+        return
+    save_x.wait()
+    own_c.wait()
+    for slot, peer in enumerate(peer_order(me, splits, True)):
+        x_copy(peer, slot).wait_send()
+        c_copy(peer, slot).wait_send()
+        send(cotangent.at[me], cot_out.at[peer], c_sent.at[slot], c_land.at[peer], "seq", peer).wait_recv()
+
+
+def forward(splits, solo, lengths, inputs, cotangent, small, weights):
+    rows, span, width = inputs.shape
+    total = splits * span
+    hidden = weights[2].shape[1]
+    heads = 2 * width // LANES
+    anyspace = pl.BlockSpec(memory_space=pl.ANY)
+    vmem = pl.BlockSpec(memory_space=pltpu.VMEM)
+    bf, f32 = jnp.bfloat16, jnp.float32
+    shapes = [
+        ((splits, span, width), bf),
+        ((splits, span, width), bf),
+        ((total, width), bf),
+        ((heads, total, LANES), bf),
+        ((heads, total, LANES), bf),
+        ((heads, total, LANES), bf),
+        ((heads // 2, total, LANES), bf),
+        ((total, width), f32),
+        ((total, width), bf),
+        ((total, hidden), bf),
+        ((total, hidden), bf),
+        ((total, LANES), bf),
+    ]
+    dma = pltpu.SemaphoreType.DMA
+    tiles = total // TILE
+    return pl.pallas_call(
+        lambda *refs: forward_kernel(splits, solo, *refs),
+        out_shape=[jax.ShapeDtypeStruct(s, d) for s, d in shapes],
+        in_specs=[pl.BlockSpec(memory_space=pltpu.SMEM)] + [anyspace] * 6 + [vmem] * len(small),
+        out_specs=[anyspace] * len(shapes),
+        scratch_shapes=[
+            pltpu.VMEM((splits, span, width), bf),
+            *[pltpu.VMEM(w.shape, bf) for w in weights],
+            pltpu.VMEM((heads, total, LANES), bf),
+            pltpu.VMEM((heads, total, LANES), bf),
+            pltpu.VMEM((heads, TILE, LANES), bf),
+            pltpu.VMEM((heads, TILE, LANES), bf),
+            pltpu.VMEM((heads // 2, TILE, LANES), bf),
+            pltpu.VMEM((TILE, width), f32),
+            pltpu.VMEM((TILE, width), bf),
+            pltpu.VMEM((TILE, hidden), bf),
+            pltpu.VMEM((TILE, hidden), bf),
+            pltpu.VMEM((TILE, width), bf),
+            pltpu.VMEM((TILE, LANES), bf),
+            *adapter_scratch(width, hidden),
+            dma((4,)),
+            dma((splits,)),
+            dma((splits,)),
+            dma((splits,)),
+            dma((splits,)),
+            dma((8,)),
+            dma((2 * tiles,)),
+            dma((3,)),
+        ],
+        compiler_params=pltpu.CompilerParams(
+            collective_id=None if solo else 2, has_side_effects=not solo, vmem_limit_bytes=62 * 2**20
+        ),
+        name="forward",
+    )(lengths, inputs, cotangent, *weights, *small)
+
+
+def backward_kernel(
+    splits, copies, solo,
+    lengths_ref, x_row, cot_row, out_row, qx_hbm, kx_hbm, vx_hbm, att_hbm, mid_hbm, nmid_hbm, act_hbm, slope_hbm,
+    narrow_hbm, wqkv_hbm, wo_hbm, w1_hbm, w2_hbm,
+    gain_ref, shift_ref, dm_ref, dh_ref, uq_ref, uh_ref, um_ref,
+    output, dx_out, total_ref,
+    wqkv, wo, w1, w2, kx, vx, dk, dv, x_t, cot_t, mid_t, nmid_t, act_t, slope_t, narrow_t, att_t, qx_t,
+    gx, dq, gmid, dx_s, part, aq, ap, a1, a2, bq, bp, b2, b1,
+    w_sem, t_sem, kv_sem, own_sem, f_sent, f_land, b_sent, b_land,
+    *sum_refs,
+):
+    me = 0 if solo else lax.axis_index("seq")
+    span, width = x_t.shape[1], x_t.shape[2]
+    hidden = w1.shape[1]
+    blocks = TILE // span
+    total = splits * span
+    tiles = total // TILE
+    heads = kx.shape[0]
+    half = LANES // 2
+    length = lengths_ref[me]
+    scale = half ** (-0.5)
+
+    def load_first(tile):
+        rows = pl.ds(tile * TILE, TILE)
+        pairs = (
+            (cot_row.at[pl.ds(tile * blocks, blocks)], cot_t),
+            (slope_hbm.at[rows, :], slope_t),
+            (act_hbm.at[rows, :], act_t),
+            (narrow_hbm.at[rows, :], narrow_t),
+            (mid_hbm.at[rows, :], mid_t),
+            (nmid_hbm.at[rows, :], nmid_t),
+            (att_hbm.at[:, rows, :], att_t),
+        )
+        return [pltpu.make_async_copy(a, b, t_sem.at[i]) for i, (a, b) in enumerate(pairs)]
+
+    def load_q(tile):
+        return pltpu.make_async_copy(qx_hbm.at[:, pl.ds(tile * TILE, TILE), :], qx_t, t_sem.at[7])
+
+    def load_x(tile):
+        return pltpu.make_async_copy(x_row.at[pl.ds(tile * blocks, blocks)], x_t, t_sem.at[8])
+
+    get_w2, get_w1, get_wo, get_wqkv = (
+        pltpu.make_async_copy(source, target, w_sem.at[index])
+        for index, (source, target) in enumerate(((w2_hbm, w2), (w1_hbm, w1), (wo_hbm, wo), (wqkv_hbm, wqkv)))
+    )
+    get_k = pltpu.make_async_copy(kx_hbm, kx, kv_sem.at[0])
+    get_v = pltpu.make_async_copy(vx_hbm, vx, kv_sem.at[1])
+    own_f = pltpu.make_async_copy(out_row.at[me], output.at[me], own_sem.at[0])
+    own_b = pltpu.make_async_copy(dx_s.at[me], dx_out.at[me], own_sem.at[1])
+
+    first = load_first(tiles - 1)
+    first[0].start()
+    get_w2.start()
+    for load in first[1:4]:
+        load.start()
+    get_w1.start()
+    for load in first[4:]:
+        load.start()
+    get_wo.start()
+    load_q(tiles - 1).start()
+    get_k.start()
+    get_v.start()
+    get_wqkv.start()
+    load_x(tiles - 1).start()
+    if not solo:
+        greet((("seq", splits), ("dp", copies)))
+        own_f.start()
+        for slot, peer in enumerate(peer_order(me, splits, True)):
+            send(out_row.at[peer], output.at[me], f_sent.at[slot], f_land.at[me], "seq", peer).start()
+    fill_adapters(dm_ref, dh_ref, uq_ref, uh_ref, um_ref, aq, ap, a1, a2, bq, bp, b2, b1)
+    part[...] = jnp.zeros_like(part)
+
+    lane = lax.broadcasted_iota(jnp.int32, (TILE, LANES), 1)
+    row = lax.broadcasted_iota(jnp.int32, (TILE, TILE), 0)
+    col = lax.broadcasted_iota(jnp.int32, (TILE, TILE), 1)
+    causal = row <= col
+    zero = jnp.zeros((TILE, LANES), jnp.bfloat16)
+    owns = (lane < half, lane >= half)
+    spares = (half, 0)
+
+    def add_upper(start, value):
+        part[0:RANK, start : start + value.shape[1]] += value
+
+    def add_lower(start, value):
+        part[RANK : 2 * RANK, start : start + value.shape[1]] += value
+
+    def b_copy(block):
+        return send(dx_s.at[block], dx_out.at[me], b_sent.at[block], b_land.at[me], "seq", block)
+
+    for tile in reversed(range(tiles)):
+        begin, end = tile * TILE, (tile + 1) * TILE
+        newest = tile == tiles - 1
+        for load in load_first(tile):
+            load.wait()
+        if newest:
+            get_w2.wait()
+            get_w1.wait()
+        spot = begin + lax.broadcasted_iota(jnp.int32, (TILE, width), 0)
+        given = cot_t[...].reshape(TILE, width)
+        gout = jnp.where(spot < length, given, jnp.zeros_like(given))
+        narrow_q = narrow_t[:, 0:RANK]
+        narrow_p = narrow_t[:, RANK : 2 * RANK]
+        narrow_1 = narrow_t[:, 2 * RANK : 3 * RANK]
+        narrow_2 = narrow_t[:, 3 * RANK : 4 * RANK]
+        gn2 = low(dotf(gout, b2[...], NT))
+        add_upper(7 * width, dotf(narrow_2, gout, TN))
+        size = 512
+
+        def contract(start):
+            return dotf(gout, w2[start : start + size, :], NT) + dotf(gn2, a2[:, start : start + size])
+
+        gnorm = jnp.zeros((TILE, width), jnp.float32)
+        gn1 = jnp.zeros((TILE, RANK), jnp.float32)
+        ahead = contract(0)
+        for start in range(0, hidden, size):
+            stop = start + size
+            gact = ahead
+            if stop < hidden:
+                ahead = contract(stop)
+            gbefore = low(gact * wide(slope_t[:, start:stop]))
+            add_lower(start, dotf(gn2, act_t[:, start:stop], TN))
+            add_lower(hidden + start, dotf(narrow_1, gbefore, TN))
+            gn1 = gn1 + dotf(gbefore, b1[:, start:stop], NT)
+            gnorm = gnorm + dotf(gbefore, w1[:, start:stop], NT)
+        gn1 = low(gn1)
+        gnorm = gnorm + dotf(gn1, a1[...])
+        add_upper(2 * width, dotf(gn1, nmid_t[...], TN))
+        unit, scaled = norm_parts(mid_t[...])
+        grad = wide(gout) + norm_back(gnorm, unit, scaled, wide(gain_ref[1:2, :]))
+        gmid[...] = grad
+        glow = low(grad)
+        if newest:
+            get_wo.wait()
+        gnp = low(dotf(glow, bp[...], NT))
+        add_upper(6 * width, dotf(narrow_p, glow, TN))
+        gatt = low(dotf(glow, wo[...], NT) + dotf(gnp, ap[...]))
+        attended = jnp.concatenate([att_t[index] for index in range(heads // 2)], axis=1)
+        add_upper(width, dotf(gnp, attended, TN))
+        for index in range(heads // 2):
+            piece = gatt[:, index * LANES : (index + 1) * LANES]
+            product = wide(piece) * wide(att_t[index])
+            for parity in range(2):
+                own, spare = owns[parity], spares[parity]
+                delta = -jnp.sum(jnp.where(own, product, 0.0), axis=-1, keepdims=True)
+                high, middle, rest = triple(jnp.broadcast_to(delta, (TILE, LANES)))
+                extra = jnp.where(
+                    lane == spare, high, jnp.where(lane == spare + 1, middle, jnp.where(lane == spare + 2, rest, zero))
+                )
+                gx[2 * index + parity] = jnp.where(own, piece, extra)
+        if tile:
+            for load in load_first(tile - 1):
+                load.start()
+        load_q(tile).wait()
+        if newest:
+            get_k.wait()
+            get_v.wait()
+
+        def attend(index, carry):
+            def products(unit):
+                head = index * GROUP + unit
+                return (
+                    dotf(kx[head, 0:end, :], qx_t[head], NT),
+                    dotf(vx[head, 0:end, :], gx[head], NT),
+                )
+
+            def spread(unit, scores, dprob):
+                head = index * GROUP + unit
+                weights = jnp.exp2(scores * LOG2E)
+                last = jnp.where(causal, weights[begin:], 0.0)
+                weights = jnp.concatenate([weights[:begin], last], axis=0) if begin else last
+                dscore = low(weights * dprob)
+                return (
+                    dotf(dscore, kx[head, 0:end, :], TN),
+                    dotf(dscore, qx_t[head]),
+                    dotf(low(weights), gx[head]),
+                )
+
+            ahead = products(0)
+            results = []
+            for unit in range(GROUP):
+                given = ahead
+                if unit + 1 < GROUP:
+                    ahead = products(unit + 1)
+                results.append(spread(unit, *given))
+            first_lanes = lax.broadcasted_iota(jnp.int32, (end, LANES), 1) < half
+            for unit in range(0, GROUP, 2):
+                pair = index * (GROUP // 2) + unit // 2
+                even, odd = results[unit], results[unit + 1]
+                dq[pair] = low(jnp.where(owns[0], even[0], odd[0]) * scale)
+                more_k = jnp.where(first_lanes, even[1], odd[1])
+                more_v = jnp.where(first_lanes, even[2], odd[2])
+                if newest:
+                    dk[pair] = more_k
+                    dv[pair] = more_v
+                else:
+                    dk[pair, 0:end, :] += more_k
+                    dv[pair, 0:end, :] += more_v
+            return carry
+
+        lax.fori_loop(0, heads // GROUP, attend, 0)
+        if tile:
+            load_q(tile - 1).start()
+        load_x(tile).wait()
+        if newest:
+            get_wqkv.wait()
+        pairs = range(heads // 2)
+        parts = [
+            jnp.concatenate([dq[index] for index in pairs], axis=1),
+            jnp.concatenate([low(dk[index, begin:end, :]) for index in pairs], axis=1),
+            jnp.concatenate([low(dv[index, begin:end, :]) for index in pairs], axis=1),
+        ]
+        gnq = jnp.zeros((TILE, RANK), jnp.float32)
+        gnormed = jnp.zeros((TILE, width), jnp.float32)
+        for index, value in enumerate(parts):
+            start, stop = index * width, (index + 1) * width
+            gnq = gnq + dotf(value, bq[:, start:stop], NT)
+            add_upper(3 * width + start, dotf(narrow_q, value, TN))
+            gnormed = gnormed + dotf(value, wqkv[:, start:stop], NT)
+        gnq = low(gnq)
+        gnormed = gnormed + dotf(gnq, aq[...])
+        unit, scaled = norm_parts(wide(x_t[...].reshape(TILE, width)))
+        normed = low(unit * wide(gain_ref[0:1, :]) + wide(shift_ref[0:1, :]))
+        add_upper(0, dotf(gnq, normed, TN))
+        dx = low(gmid[...] + norm_back(gnormed, unit, scaled, wide(gain_ref[0:1, :])))
+        dx_s[tile * blocks : (tile + 1) * blocks] = dx.reshape(blocks, span, width)
+        if tile:
+            load_x(tile - 1).start()
+        if not solo:
+            for block in range(tile * blocks, (tile + 1) * blocks):
+
+                @pl.when(me != block)
+                def _():
+                    b_copy(block).start()
+
+                @pl.when(me == block)
+                def _():
+                    own_b.start()
+
+    part[0:RANK, 3 * width :] = ADAPTER_SCALE * part[0:RANK, 3 * width :]
+    part[RANK : 2 * RANK, hidden:] = ADAPTER_SCALE * part[RANK : 2 * RANK, hidden:]
+    if solo:
+        total_ref[...] = part[...]
+        return
+    sum_everywhere(splits, copies, part, total_ref, *sum_refs)
+    own_f.wait()
+    own_b.wait()
+    for slot, peer in enumerate(peer_order(me, splits, True)):
+        send(out_row.at[peer], output.at[peer], f_sent.at[slot], f_land.at[peer], "seq", peer).wait()
+        send(dx_s.at[peer], dx_out.at[peer], b_sent.at[peer], b_land.at[peer], "seq", peer).wait()
+
+
+def backward(splits, copies, solo, lengths, saved, weights, small):
+    span, width = saved[0].shape[1:]
+    hidden = weights[2].shape[1]
+    total = splits * span
+    heads = saved[3].shape[0]
+    blocks = TILE // span
+    anyspace = pl.BlockSpec(memory_space=pl.ANY)
+    vmem = pl.BlockSpec(memory_space=pltpu.VMEM)
+    bf, f32 = jnp.bfloat16, jnp.float32
+    dma = pltpu.SemaphoreType.DMA
+    scratch = [
+        *[pltpu.VMEM(w.shape, bf) for w in weights],
+        pltpu.VMEM((heads, total, LANES), bf),
+        pltpu.VMEM((heads, total, LANES), bf),
+        pltpu.VMEM((heads // 2, total, LANES), f32),
+        pltpu.VMEM((heads // 2, total, LANES), f32),
+        pltpu.VMEM((blocks, span, width), bf),
+        pltpu.VMEM((blocks, span, width), bf),
+        pltpu.VMEM((TILE, width), f32),
+        pltpu.VMEM((TILE, width), bf),
+        pltpu.VMEM((TILE, hidden), bf),
+        pltpu.VMEM((TILE, hidden), bf),
+        pltpu.VMEM((TILE, LANES), bf),
+        pltpu.VMEM((heads // 2, TILE, LANES), bf),
+        pltpu.VMEM((heads, TILE, LANES), bf),
+        pltpu.VMEM((heads, TILE, LANES), bf),
+        pltpu.VMEM((heads // 2, TILE, LANES), bf),
+        pltpu.VMEM((TILE, width), f32),
+        pltpu.VMEM((splits, span, width), bf),
+        pltpu.VMEM((2 * RANK, 8 * width), f32),
+        *adapter_scratch(width, hidden),
+        dma((4,)),
+        dma((9,)),
+        dma((2,)),
+        dma((2,)),
+        dma((splits,)),
+        dma((splits,)),
+        dma((splits,)),
+        dma((splits,)),
+    ]
+    if not solo:
+        scratch += sum_scratch(splits, copies, 8 * width)
+    return pl.pallas_call(
+        lambda *refs: backward_kernel(splits, copies, solo, *refs),
+        out_shape=[
+            jax.ShapeDtypeStruct((splits, span, width), bf),
+            jax.ShapeDtypeStruct((splits, span, width), bf),
+            jax.ShapeDtypeStruct((2 * RANK, 8 * width), f32),
+        ],
+        in_specs=[pl.BlockSpec(memory_space=pltpu.SMEM)]
+        + [anyspace] * (len(saved) + len(weights))
+        + [vmem] * len(small),
+        out_specs=[anyspace, anyspace, vmem],
+        scratch_shapes=scratch,
+        compiler_params=pltpu.CompilerParams(
+            collective_id=None if solo else 3, has_side_effects=not solo, vmem_limit_bytes=63 * 2**20
+        ),
+        name="backward",
+    )(lengths, *saved, *weights, *small)
+
+
+def local_by_heads(
     inputs,
     cotangent,
     lengths,
@@ -340,6 +1256,81 @@
     )
 
 
+def local_by_rows(
+    pieces,
+    copies,
+    inputs,
+    cotangent,
+    lengths,
+    norm_gain,
+    norm_shift,
+    query_key_value_weight,
+    output_projection_weight,
+    first_feedforward_weight,
+    second_feedforward_weight,
+    biases,
+    down_model,
+    down_hidden,
+    query_key_value_upward,
+    hidden_adapter_upward,
+    model_adapter_upward,
+    row_down_model,
+    col_down_model,
+    row_down_hidden,
+    col_down_hidden,
+    row_up_qkv,
+    col_up_qkv,
+    row_up_hidden,
+    col_up_hidden,
+    row_up_model,
+    col_up_model,
+):
+    flip = lambda array: jnp.swapaxes(array, -1, -2)
+    adapters = [
+        flip(down_model),
+        flip(down_hidden),
+        query_key_value_upward,
+        hidden_adapter_upward,
+        model_adapter_upward,
+    ]
+    norms = [norm_gain, norm_shift]
+    weights = [
+        query_key_value_weight,
+        output_projection_weight,
+        first_feedforward_weight,
+        second_feedforward_weight,
+    ]
+    saved = list(forward(
+        pieces, False, lengths, inputs, cotangent, [biases.reshape(1, -1)] + norms + adapters, weights
+    ))
+    saved[2] = saved[2].reshape(inputs.shape)
+    output, input_grad, total = backward(
+        pieces, copies, False, lengths, saved, weights, norms + adapters
+    )
+    return update(
+        total,
+        output,
+        input_grad,
+        adapters,
+        row_down_model,
+        col_down_model,
+        row_down_hidden,
+        col_down_hidden,
+        row_up_qkv,
+        col_up_qkv,
+        row_up_hidden,
+        col_up_hidden,
+        row_up_model,
+        col_up_model,
+    )
+
+
+def local(pieces, copies, inputs, *others):
+    if inputs.shape[0] == pieces and TILE % inputs.shape[1] == 0:
+        return local_by_rows(pieces, copies, inputs, *others)
+    return local_by_heads(inputs, *others)
+
+
 def solution(mesh):
     placed = (
         P("dp", "seq", None),
@@ -369,7 +1360,7 @@
         P(),
     )
     return jax.shard_map(
-        local,
+        partial(local, mesh.shape["seq"], mesh.shape["dp"]),
         mesh=mesh,
         in_specs=placed,
         out_specs=(

time: 1210 us -> 279 us (0.23); the launches traced: 1190 us -> 277 us
  waiting for transfers between devices: 469 us -> 0 us
  Pallas kernels: 0 us -> 270 us
  matrix products: 263 us -> 0 us
  local copies, waits for them, and re-layouts: 224 us -> 5.57 us
  other arithmetic: 195 us -> 0 us
  between operations: 21.7 us -> 1.17 us
  starting transfers between devices: 20.1 us -> 0 us
    pallas_call x0 -> x3, Pallas kernels: none -> 270 us  [the longest x1 134 us: backward(): pl.pallas_call(lambda *refs: backward_kernel(splits, copies, solo, *refs)...]
    dot_general x144 -> x0, matrix products: 263 us -> none  [the longest x12 74.2 us: compared_with(): jnp.einsum('tc,rc->tr', left, right, preferred_element_type=jnp.float32)]
    psum x2 -> x0, waiting for transfers between devices: 251 us -> none  [local(): lax.psum((jnp.stack([grad_down_qkv, grad_down_proj, grad_down_expand]), g...]
    all_to_all x4 -> x0, waiting for transfers between devices: 217 us -> none  [the longest x1 139 us: local(): lax.all_to_all(mixed_rows, 'seq', split_axis=3, concat_axis=1, tiled=True)]
    sub x13 -> x0, other arithmetic: 77.9 us -> none  [the longest x8 74.6 us: attend_back(): dscore = (probs * (dprob - delta)).astype(jnp.bfloat16)]
    unnamed x190 -> x36, local copies, waits for them, and re-layouts: 59 us -> 4.22 us
    all_to_all x6 -> x0, local copies, waits for them, and re-layouts: 54.6 us -> none  [the longest x1 21.4 us: local(): lax.all_to_all(as_sent(grad_triple), 'seq', split_axis=1, concat_axis=3,...]
    while x34 -> x0, local copies, waits for them, and re-layouts: 41.6 us -> none  [the longest x1 30.6 us: local(): lax.map(partial(head_backward, False), (by_head, grad_heads, lse, lengths))]
  transfers between devices with their start and end apart: 6 -> 0, of which waited for: 5 -> 0; matrix products, arithmetic and copies ran while one was open for 6% -> 0% of each run, Pallas kernels for 0% -> 0%
where the time goes in v2:
time: 279 us; the launch traced here: 277 us
  Pallas kernels  270 us (97%)
  local copies, waits for them, and re-layouts  5.57 us (2%)
    pallas_call x1, Pallas kernels, backward(): pl.pallas_call(lambda *refs: backward_kernel(splits, copies, solo, *refs)...  134 us
    pallas_call x1, Pallas kernels, forward(): pl.pallas_call(lambda *refs: forward_kernel(splits, solo, *refs), out_sha...  132 us

profile of v2, /device:TPU:0, one launch (start us, length us, event | category | flops | bytes accessed | tf_op | source)
XLA Modules:
  0.0 276.5 jit_solution(1196663911265378529)
XLA Ops:
  0.7 1.4 reshape.86.refs_7_
  2.0 132.2 %forward.1 = (bf16[8,128,1024]{2,1,0:T(8,128)(2,1)}, bf16[8,128,1024]{2,1,0:T(8,128)(2,1)}, bf16[1024,1024]{1,0:T(8,128)(2,1)}, bf16[16,1024,128]{2,1,0:T(8,128)...) custom-call(s32[8]{0:T(128)} %refs_0_.3, ...), custom_call_target="tpu_custom_call" | custom-call | tf_op jit(solution)/shard_map/forward/pallas_call | solution.py:754
  134.3 0.0 copy-start.2
  134.3 0.0 copy-start.3
  134.3 0.0 copy-start.4
  134.3 0.0 copy-start.5
  134.3 0.0 copy-start.6
  134.3 0.0 copy-start.8
  134.3 0.0 copy-start.9
  134.3 0.0 copy-start.10
  134.4 0.0 copy-start.11
  134.4 0.0 copy-start.12
  134.4 0.0 copy-start.13
  134.4 0.0 copy-start.14
  134.4 0.0 copy-start.15
  134.4 0.0 copy-start.16
  134.4 0.0 copy-start.17
  134.4 134.4 %backward.1 = (bf16[8,128,1024]{2,1,0:T(8,128)(2,1)}, bf16[8,128,1024]{2,1,0:T(8,128)(2,1)}, f32[8,8192]{1,0:T(8,128)}) custom-call(s32[8]{0:T(128)} %refs_0_.3, bf16[8,128,1024]{2,1,0:T(8,128)(2,1)} %get-tuple-element.59.refs_1_, bf16[8,128,1024]{2,1,0:T(8,128)(2,1)} %get-tuple-element.60.refs_2_, bf16[8,128,1024]{2,1,0:T(8,128)(2,1)} %bitcast.31, ...), custom_call_target="tpu_custom_call" | custom-call | tf_op jit(solution)/shard_map/backward/pallas_call | solution.py:1083
  268.9 0.0 copy-done.2
  268.9 0.0 copy-done.3
  268.9 0.0 copy-done.4
  268.9 0.0 copy-done.5
  268.9 0.0 copy-done.6
  268.9 0.0 copy-done.8
  268.9 0.0 copy-done.9
  268.9 0.0 copy-done.10
  268.9 0.0 copy-done.11
  269.0 0.0 copy-done.12
  269.0 1.6 copy-done
  270.6 1.6 copy-done.1
  272.2 0.9 copy-done.7
  273.1 3.1 %factored_update.1 = (bf16[8,128,1024]{2,1,0:T(8,128)(2,1)}, bf16[8,128,1024]{2,1,0:T(8,128)(2,1)}, f32[3,4,1024]{2,1,0:T(4,128)}, f32[4,4096]{1,0:T(4,128)}, f3...) custom-call(f32[8,8192]{1,0:T(8,128)S(1)} %copy-done.7, ...), custom_call_target="tpu_custom_call" | custom-call | tf_op jit(solution)/shard_map/factored_update/pallas_call | solution.py:427
  (8 shorter events, 0.0 us)
Async XLA Ops:
  134.3 134.6 %copy-start.2 = (f32[4096,4]{0,1:T(4,128)S(1)}, f32[4096,4]{0,1:T(4,128)}, u32[]{:S(2)}) copy-start(f32[4096,4]{0,1:T(4,128)} %param.36) | copy-start | bytes 196612
  134.3 134.6 %copy-start.3 = (f32[4,4096]{1,0:T(4,128)S(1)}, f32[4,4096]{1,0:T(4,128)}, u32[]{:S(2)}) copy-start(f32[4,4096]{1,0:T(4,128)} %uh.1) | copy-start | bytes 196612
  134.3 134.6 %copy-start.4 = (f32[3,1024,4]{1,2,0:T(4,128)S(1)}, f32[3,1024,4]{1,2,0:T(4,128)}, u32[]{:S(2)}) copy-start(f32[3,1024,4]{1,2,0:T(4,128)} %param.35) | copy-start | bytes 147460
  134.3 134.6 %copy-start.5 = (f32[4,3072]{1,0:T(4,128)S(1)}, f32[4,3072]{1,0:T(4,128)}, u32[]{:S(2)}) copy-start(f32[4,3072]{1,0:T(4,128)} %uq.1) | copy-start | bytes 147460
  134.3 134.6 %copy-start.6 = (f32[2,4,1024]{2,1,0:T(4,128)S(1)}, f32[2,4,1024]{2,1,0:T(4,128)}, u32[]{:S(2)}) copy-start(f32[2,4,1024]{2,1,0:T(4,128)} %um.1) | copy-start | bytes 98308
  134.3 134.6 %copy-start.8 = (f32[3,1024]{1,0:T(4,128)S(1)}, f32[3,1024]{1,0:T(4,128)}, u32[]{:S(2)}) copy-start(f32[3,1024]{1,0:T(4,128)} %row_dm.1) | copy-start | bytes 36868
  134.3 134.6 %copy-start.9 = (f32[4096]{0:T(1024)S(1)}, f32[4096]{0:T(1024)}, u32[]{:S(2)}) copy-start(f32[4096]{0:T(1024)} %param.42) | copy-start | bytes 49156
  134.3 134.6 %copy-start.10 = (f32[4096]{0:T(1024)S(1)}, f32[4096]{0:T(1024)}, u32[]{:S(2)}) copy-start(f32[4096]{0:T(1024)} %param.47) | copy-start | bytes 49156
  134.4 134.6 %copy-start.11 = (f32[3072]{0:T(1024)S(1)}, f32[3072]{0:T(1024)}, u32[]{:S(2)}) copy-start(f32[3072]{0:T(1024)} %param.45) | copy-start | bytes 36868
  134.4 134.6 %copy-start.12 = (f32[2,1024]{1,0:T(2,128)S(1)}, f32[2,1024]{1,0:T(2,128)}, u32[]{:S(2)}) copy-start(f32[2,1024]{1,0:T(2,128)} %col_um.1) | copy-start | bytes 24580
  134.4 134.6 %copy-start.13 = (f32[3,4]{1,0:T(4,128)S(1)}, f32[3,4]{1,0:T(4,128)}, u32[]{:S(2)}) copy-start(f32[3,4]{1,0:T(4,128)} %col_dm.1) | copy-start | bytes 148
  134.4 134.6 %copy-start.14 = (f32[2,4]{1,0:T(2,128)S(1)}, f32[2,4]{1,0:T(2,128)}, u32[]{:S(2)}) copy-start(f32[2,4]{1,0:T(2,128)} %row_um.1) | copy-start | bytes 100
  134.4 134.6 %copy-start.15 = (f32[4]{0:T(128)S(1)}, f32[4]{0:T(128)}, u32[]{:S(2)}) copy-start(f32[4]{0:T(128)} %param.43) | copy-start | bytes 52
  134.4 134.6 %copy-start.16 = (f32[4]{0:T(128)S(1)}, f32[4]{0:T(128)}, u32[]{:S(2)}) copy-start(f32[4]{0:T(128)} %param.44) | copy-start | bytes 52
  134.4 134.6 %copy-start.17 = (f32[4]{0:T(128)S(1)}, f32[4]{0:T(128)}, u32[]{:S(2)}) copy-start(f32[4]{0:T(128)} %param.46) | copy-start | bytes 52
  269.0 1.6 copy-start
  270.6 1.6 copy-start.1
  272.2 0.9 copy-start.7

commit v3 on v2

--- a/solution.py
+++ b/solution.py
@@ -434,7 +434,7 @@
             pltpu.VMEM(output.shape, output.dtype),
             pltpu.SemaphoreType.DMA((2,)),
         ],
-        compiler_params=pltpu.CompilerParams(vmem_limit_bytes=24 * 2**20),
+        compiler_params=pltpu.CompilerParams(vmem_limit_bytes=60 * 2**20),
         name="factored_update",
     )(total, output, input_grad, *adapters, *given)
     results = list(results)
@@ -446,19 +446,6 @@
     return tuple(results)
 
 
-TILE = 256
-GROUP = 4
-LANES = 128
-
-
-def peer_order(me, splits, far_first):
-    half = splits // 2
-    side, place = me // half, lax.rem(me, half)
-    far = [(1 - side) * half + lax.rem(place + shift, half) for shift in range(half)]
-    near = [side * half + lax.rem(place + shift, half) for shift in range(1, half)]
-    return far + near if far_first else near + far
-
-
 def fill_adapters(dm_ref, dh_ref, uq_ref, uh_ref, um_ref, aq, ap, a1, a2, bq, bp, b2, b1):
     for index, ref in enumerate((aq, ap, a1)):
         ref[...] = low(dm_ref[index])
@@ -472,164 +459,254 @@
     return [pltpu.VMEM((RANK, size), jnp.bfloat16) for size in sizes]
 
 
-def forward_kernel(
-    splits, solo,
+TILE = 256
+GROUP = 4
+LANES = 128
+
+
+def peer_order(me, splits):
+    half = splits // 2
+    side, place = me // half, lax.rem(me, half)
+    far = [(1 - side) * half + lax.rem(place + shift, half) for shift in range(half)]
+    near = [side * half + lax.rem(place + shift, half) for shift in range(1, half)]
+    return far, near
+
+
+def block_kernel(
+    splits, copies, solo,
     lengths_ref, inputs, cotangent, wqkv_hbm, wo_hbm, w1_hbm, w2_hbm,
     bias_ref, gain_ref, shift_ref, dm_ref, dh_ref, uq_ref, uh_ref, um_ref,
-    x_out, cot_out, out_out, qx_out, kx_out, vx_out, att_out, mid_out, nmid_out, act_out, slope_out, narrow_out,
-    xr, wqkv, wo, w1, w2, kx, vx, qs, qb, att, mid, nmid, act, slope, outs, narrow,
+    output, dx_out, total_ref, cot_in, out_row, att_hbm, mid_hbm, act_hbm, slope_hbm,
+    wqkv, wo, w1, w2, kx, vx, qx, dk, dv, xr, att, mid, act, slope, cot_t, outs, gx, dq, narrow, part,
     aq, ap, a1, a2, bq, bp, b2, b1,
-    w_sem, x_sent, x_land, c_sent, c_land, o_sem, kv_sem, own_sem,
+    w_sem, s_sem, l_sem, own_sem, x_sent, x_land, c_sent, c_land, f_sent, f_land, b_sent, b_land,
+    *sum_refs,
 ):
     me = 0 if solo else lax.axis_index("seq")
     span, width = xr.shape[1], xr.shape[2]
+    hidden = w1.shape[1]
     total = splits * span
-    hidden = w1.shape[1]
+    tiles = total // TILE
     blocks = TILE // span
     heads = kx.shape[0]
+    pairs = heads // 2
     half = LANES // 2
     length = lengths_ref[me]
+    upper = me >= splits // 2
+
     loads = [
         pltpu.make_async_copy(source, target, w_sem.at[index])
         for index, (source, target) in enumerate(((wqkv_hbm, wqkv), (wo_hbm, wo), (w1_hbm, w1), (w2_hbm, w2)))
     ]
-    own_x = pltpu.make_async_copy(inputs.at[me], xr.at[me], own_sem.at[0])
-    own_c = pltpu.make_async_copy(cotangent.at[me], cot_out.at[me], own_sem.at[1])
-    save_x = pltpu.make_async_copy(xr, x_out, own_sem.at[2])
-    if not solo:
-        greet((("seq", splits),))
-        own_x.start()
-    else:
-        all_x = pltpu.make_async_copy(inputs, xr, own_sem.at[0])
-        all_x.start()
-    loads[0].start()
+    own_x = pltpu.make_async_copy(inputs if solo else inputs.at[me], xr if solo else xr.at[me], own_sem.at[0])
+    own_b = pltpu.make_async_copy(xr.at[me], dx_out.at[me], own_sem.at[1])
+
+    def saves(tile):
+        rows = pl.ds(tile * TILE, TILE)
+        moves = (
+            (att, att_hbm.at[:, rows, :]),
+            (mid, mid_hbm.at[rows, :]),
+            (act, act_hbm.at[rows, :]),
+            (slope, slope_hbm.at[rows, :]),
+            (outs, out_row.at[pl.ds(tile * blocks, blocks)]),
+        )
+        return [pltpu.make_async_copy(a, b, s_sem.at[i]) for i, (a, b) in enumerate(moves)]
+
+    def fetches(tile):
+        rows = pl.ds(tile * TILE, TILE)
+        moves = (
+            (slope_hbm.at[rows, :], slope),
+            (act_hbm.at[rows, :], act),
+            (att_hbm.at[:, rows, :], att),
+            (mid_hbm.at[rows, :], mid),
+        )
+        return [pltpu.make_async_copy(a, b, l_sem.at[i]) for i, (a, b) in enumerate(moves)]
 
     def x_copy(peer, slot):
         return send(inputs.at[peer], xr.at[me], x_sent.at[slot], x_land.at[me], "seq", peer)
 
     def c_copy(peer, slot):
-        return send(cotangent.at[peer], cot_out.at[me], c_sent.at[slot], c_land.at[me], "seq", peer)
+        return send(cotangent.at[peer], cot_in.at[me], c_sent.at[slot], c_land.at[me], "seq", peer)
+
+    def f_copy(block):
+        return send(out_row.at[block], output.at[me], f_sent.at[block], f_land.at[me], "seq", block)
+
+    def b_copy(block):
+        return send(xr.at[block], dx_out.at[me], b_sent.at[block], b_land.at[me], "seq", block)
+
+    def tile_blocks(tile):
+        return range(tile * blocks, (tile + 1) * blocks)
+
+    def cot_move(block, fetched):
+        slot = cot_t.at[block % blocks]
+        source = cotangent.at[me] if fetched else cot_in.at[block]
+        return pltpu.make_async_copy(source, slot, l_sem.at[4 + block % blocks])
+
+    def cot_fetch(tile):
+        if solo:
+            for block in tile_blocks(tile):
+                cot_move(block, False).start()
+            return
+        for block in tile_blocks(tile):
+
+            @pl.when(me == block)
+            def _():
+                cot_move(block, True).start()
+
+            @pl.when(me != block)
+            def _():
+                send(cotangent.at[block], cot_in.at[block], c_sent.at[0], c_land.at[block], "seq", block).wait_recv()
+                cot_move(block, False).start()
+
+    def x_wait(tile):
+        if solo:
+            return
+        for block in tile_blocks(tile):
+
+            @pl.when(me != block)
+            def _():
+                send(inputs.at[block], xr.at[block], x_sent.at[0], x_land.at[block], "seq", block).wait_recv()
+
+    def send_output(tile):
+        if solo:
+            return
+        for block in tile_blocks(tile):
+
+            @pl.when(me != block)
+            def _():
+                f_copy(block).start()
 
     if not solo:
-        pair = me // 2
-        outward = jnp.logical_or(pair == 0, pair == splits // 2 - 2)
+        greet((("seq", splits), ("dp", copies)))
+    own_x.start()
+    loads[0].start()
+    if not solo:
+        far, near = peer_order(me, splits)
+        quarter = lax.rem(me, splits // 2) // 2
+        outward = jnp.logical_or(
+            jnp.logical_and(me < splits // 2, quarter == 0), jnp.logical_and(upper, quarter == 0)
+        )
 
         @pl.when(outward)
         def _():
-            for slot, peer in enumerate(peer_order(me, splits, True)):
+            for slot, peer in enumerate(far + near):
                 x_copy(peer, slot).start()
 
         @pl.when(jnp.logical_not(outward))
         def _():
-            for slot, peer in enumerate(peer_order(me, splits, False)):
+            for slot, peer in enumerate(near + far):
                 x_copy(peer, slot).start()
 
     for load in loads[1:]:
         load.start()
     fill_adapters(dm_ref, dh_ref, uq_ref, uh_ref, um_ref, aq, ap, a1, a2, bq, bp, b2, b1)
-    if solo:
-        all_x.wait()
-    else:
-        own_x.wait()
+    part[...] = jnp.zeros_like(part)
 
     lane = lax.broadcasted_iota(jnp.int32, (TILE, LANES), 1)
     row = lax.broadcasted_iota(jnp.int32, (TILE, TILE), 0)
     col = lax.broadcasted_iota(jnp.int32, (TILE, TILE), 1)
-    causal = col <= row
     zero = jnp.zeros((TILE, LANES), jnp.bfloat16)
     one = jnp.ones((TILE, LANES), jnp.bfloat16)
-    scale = jnp.asarray(half ** (-0.5), jnp.bfloat16)
+    scale = half ** (-0.5)
     owns = (lane < half, lane >= half)
     spares = (half, 0)
 
+    def with_extra(own, spare, value, extra):
+        high, middle, rest = triple(extra)
+        return jnp.where(
+            own,
+            value,
+            jnp.where(lane == spare, high, jnp.where(lane == spare + 1, middle, jnp.where(lane == spare + 2, rest, zero))),
+        )
+
     def bias(start, size):
         return wide(bias_ref[0:1, start : start + size])
 
-    def saves(tile):
-        rows = pl.ds(tile * TILE, TILE)
-        return [
-            pltpu.make_async_copy(source, target, o_sem.at[index])
-            for index, (source, target) in enumerate(
-                (
-                    (qb, qx_out.at[:, rows, :]),
-                    (att, att_out.at[:, rows, :]),
-                    (mid, mid_out.at[rows, :]),
-                    (nmid, nmid_out.at[rows, :]),
-                    (act, act_out.at[rows, :]),
-                    (slope, slope_out.at[rows, :]),
-                    (outs, out_out.at[rows, :]),
-                    (narrow, narrow_out.at[rows, :]),
-                )
-            )
-        ]
-
-    def kv_saves(tile):
-        rows = pl.ds(tile * TILE, TILE)
-        return [
-            pltpu.make_async_copy(kx.at[:, rows, :], kx_out.at[:, rows, :], kv_sem.at[2 * tile]),
-            pltpu.make_async_copy(vx.at[:, rows, :], vx_out.at[:, rows, :], kv_sem.at[2 * tile + 1]),
-        ]
-
-    tiles = total // TILE
-    for tile in range(tiles):
-        begin, end = tile * TILE, (tile + 1) * TILE
-        for block in range(tile * blocks, (tile + 1) * blocks):
-            if solo:
-                continue
-
-            @pl.when(me != block)
-            def _():
-                send(inputs.at[block], xr.at[block], x_sent.at[0], x_land.at[block], "seq", block).wait_recv()
-
-        if tile == tiles - 1 and not solo:
-            save_x.start()
-            own_c.start()
-            for slot, peer in enumerate(peer_order(me, splits, True)):
-                c_copy(peer, slot).start()
-        if tile == 0:
-            loads[0].wait()
-        else:
-            saves(tile - 1)[7].wait()
-        x = wide(xr[tile * blocks : (tile + 1) * blocks].reshape(TILE, width))
+    def rows_of(tile):
+        if isinstance(tile, int):
+            return pl.ds(tile * TILE, TILE)
+        return pl.ds(pl.multiple_of(tile * TILE, TILE), TILE)
+
+    def project(tile):
+        rows = rows_of(tile)
+        x = wide(xr[pl.ds(tile * blocks, blocks)].reshape(TILE, width))
         unit, _ = norm_parts(x)
         normed = low(unit * wide(gain_ref[0:1, :]) + wide(shift_ref[0:1, :]))
         narrow_q = low(dotf(normed, aq[...], NT))
-        narrow[:, 0:RANK] = narrow_q
-        spot = begin + lax.broadcasted_iota(jnp.int32, (TILE, LANES), 0)
-        valid = spot < length
-        limit = jnp.where(valid, 0.0, MASKED).astype(jnp.bfloat16)
+        narrow[rows, 0:RANK] = narrow_q
+        spot = tile * TILE + lax.broadcasted_iota(jnp.int32, (TILE, LANES), 0)
+        limit = jnp.where(spot < length, 0.0, MASKED).astype(jnp.bfloat16)
         size = 512
-        for part in range(3):
+        for index in range(3):
             for start in range(0, width, size):
-                column = part * width + start
+                column = index * width + start
                 value = dotf(normed, wqkv[:, column : column + size]) + dotf(narrow_q, bq[:, column : column + size])
-                if part == 0:
+                if index == 0:
                     value = value + bias(start, size)
-                if part == 2:
+                if index == 2:
                     value = value + bias(width + start, size)
                 value = low(value)
-                for index in range(size // LANES):
-                    piece = value[:, index * LANES : (index + 1) * LANES]
+                for pair in range(size // LANES):
+                    piece = value[:, pair * LANES : (pair + 1) * LANES]
                     for parity in range(2):
-                        head = 2 * (start // LANES + index) + parity
+                        head = 2 * (start // LANES + pair) + parity
                         own, spare = owns[parity], spares[parity]
-                        if part == 0:
-                            qs[head] = jnp.where(own, piece * scale, jnp.where(lane == spare + 3, one, zero))
-                        elif part == 1:
+                        if index == 0:
+                            extra = jnp.where(lane == spare + 3, one, zero)
+                            qx[head, rows, :] = jnp.where(own, piece * jnp.asarray(scale, jnp.bfloat16), extra)
+                        elif index == 1:
                             extra = jnp.where(lane == spare + 3, limit, jnp.where(lane < spare + 3, one, zero))
-                            kx[head, begin:end, :] = jnp.where(own, piece, extra)
+                            kx[head, rows, :] = jnp.where(own, piece, extra)
                         else:
-                            vx[head, begin:end, :] = jnp.where(own, piece, one)
-        for save in kv_saves(tile):
-            save.start()
+                            vx[head, rows, :] = jnp.where(own, piece, one)
+
+    if not solo:
+
+        @pl.when(upper)
+        def _():
+            for tile in range(tiles // 2, tiles):
+                x_wait(tile)
+
+    own_x.wait()
+    loads[0].wait()
+    if not solo:
+
+        @pl.when(upper)
+        def _():
+            lax.fori_loop(tiles // 2, tiles, lambda tile, carry: (project(tile), carry)[1], 0)
+
+    for tile in range(tiles):
+        begin, end = tile * TILE, (tile + 1) * TILE
+        if tile < tiles // 2:
+            x_wait(tile)
+            project(tile)
+        elif solo:
+            project(tile)
+        else:
+
+            @pl.when(jnp.logical_not(upper))
+            def _():
+                x_wait(tile)
+                project(tile)
+
+        if not solo:
+            ready = upper if tile == tiles // 2 - 1 else jnp.logical_not(upper)
+            if tile == tiles // 2 - 1 or tile == tiles // 2:
+
+                @pl.when(ready)
+                def _():
+                    for slot, peer in enumerate(far + near):
+                        c_copy(peer, slot).start()
+
         if tile:
-            for save in saves(tile - 1)[0:2]:
-                save.wait()
+            saves(tile - 1)[0].wait()
+        valid = begin + lax.broadcasted_iota(jnp.int32, (TILE, LANES), 0) < length
+        causal = col <= row
 
         def attend(index, carry):
             def scores(unit):
                 head = index * GROUP + unit
-                return dotf(qs[head], kx[head, 0:end, :], NT)
+                return dotf(qx[head, begin:end, :], kx[head, 0:end, :], NT)
 
             def mix(unit, value):
                 head = index * GROUP + unit
@@ -641,11 +718,7 @@
                 spare, own = spares[unit % 2], owns[unit % 2]
                 summed = mixed[:, spare : spare + 1]
                 back = jnp.where(valid, -(top + jnp.log(summed)), MASKED)
-                high, middle, rest = triple(back)
-                extra = jnp.where(
-                    lane == spare, high, jnp.where(lane == spare + 1, middle, jnp.where(lane == spare + 2, rest, zero))
-                )
-                qb[head] = jnp.where(own, qs[head], extra)
+                qx[head, begin:end, :] = with_extra(own, spare, qx[head, begin:end, :], back)
                 return mixed * (1.0 / summed)
 
             ahead = scores(0)
@@ -660,15 +733,14 @@
             return carry
 
         lax.fori_loop(0, heads // GROUP, attend, 0)
-        for save in saves(tile)[0:2]:
-            save.start()
         if tile == 0:
             for load in loads[1:]:
                 load.wait()
         else:
-            for save in saves(tile - 1)[2:7]:
+            for save in saves(tile - 1)[1:]:
                 save.wait()
-        attended = jnp.concatenate([att[index] for index in range(heads // 2)], axis=1)
+            send_output(tile - 1)
+        attended = jnp.concatenate([att[index] for index in range(pairs)], axis=1)
         narrow_p = low(dotf(attended, ap[...], NT))
         middle = (
             wide(xr[tile * blocks : (tile + 1) * blocks].reshape(TILE, width))
@@ -679,7 +751,6 @@
         mid[...] = middle
         unit, _ = norm_parts(middle)
         normed = low(unit * wide(gain_ref[1:2, :]) + wide(shift_ref[1:2, :]))
-        nmid[...] = normed
         narrow_1 = low(dotf(normed, a1[...], NT))
         size = 256
 
@@ -705,167 +776,15 @@
             result = result + dotf(active, w2[start:stop, :])
             narrow_2 = narrow_2 + dotf(active, a2[:, start:stop], NT)
         narrow_2 = low(narrow_2)
-        outs[...] = low(result + dotf(narrow_2, b2[...]))
-        narrow[:, RANK : 2 * RANK] = narrow_p
-        narrow[:, 2 * RANK : 3 * RANK] = narrow_1
-        narrow[:, 3 * RANK : 4 * RANK] = narrow_2
-        for save in saves(tile)[2:8]:
-            save.start()
-
-    for save in saves(tiles - 1):
-        save.wait()
-    for tile in range(tiles):
-        for save in kv_saves(tile):
-            save.wait()
-    if solo:
-        return
-    save_x.wait()
-    own_c.wait()
-    for slot, peer in enumerate(peer_order(me, splits, True)):
-        x_copy(peer, slot).wait_send()
-        c_copy(peer, slot).wait_send()
-        send(cotangent.at[me], cot_out.at[peer], c_sent.at[slot], c_land.at[peer], "seq", peer).wait_recv()
-
-
-def forward(splits, solo, lengths, inputs, cotangent, small, weights):
-    rows, span, width = inputs.shape
-    total = splits * span
-    hidden = weights[2].shape[1]
-    heads = 2 * width // LANES
-    anyspace = pl.BlockSpec(memory_space=pl.ANY)
-    vmem = pl.BlockSpec(memory_space=pltpu.VMEM)
-    bf, f32 = jnp.bfloat16, jnp.float32
-    shapes = [
-        ((splits, span, width), bf),
-        ((splits, span, width), bf),
-        ((total, width), bf),
-        ((heads, total, LANES), bf),
-        ((heads, total, LANES), bf),
-        ((heads, total, LANES), bf),
-        ((heads // 2, total, LANES), bf),
-        ((total, width), f32),
-        ((total, width), bf),
-        ((total, hidden), bf),
-        ((total, hidden), bf),
-        ((total, LANES), bf),
-    ]
-    dma = pltpu.SemaphoreType.DMA
-    tiles = total // TILE
-    return pl.pallas_call(
-        lambda *refs: forward_kernel(splits, solo, *refs),
-        out_shape=[jax.ShapeDtypeStruct(s, d) for s, d in shapes],
-        in_specs=[pl.BlockSpec(memory_space=pltpu.SMEM)] + [anyspace] * 6 + [vmem] * len(small),
-        out_specs=[anyspace] * len(shapes),
-        scratch_shapes=[
-            pltpu.VMEM((splits, span, width), bf),
-            *[pltpu.VMEM(w.shape, bf) for w in weights],
-            pltpu.VMEM((heads, total, LANES), bf),
-            pltpu.VMEM((heads, total, LANES), bf),
-            pltpu.VMEM((heads, TILE, LANES), bf),
-            pltpu.VMEM((heads, TILE, LANES), bf),
-            pltpu.VMEM((heads // 2, TILE, LANES), bf),
-            pltpu.VMEM((TILE, width), f32),
-            pltpu.VMEM((TILE, width), bf),
-            pltpu.VMEM((TILE, hidden), bf),
-            pltpu.VMEM((TILE, hidden), bf),
-            pltpu.VMEM((TILE, width), bf),
-            pltpu.VMEM((TILE, LANES), bf),
-            *adapter_scratch(width, hidden),
-            dma((4,)),
-            dma((splits,)),
-            dma((splits,)),
-            dma((splits,)),
-            dma((splits,)),
-            dma((8,)),
-            dma((2 * tiles,)),
-            dma((3,)),
-        ],
-        compiler_params=pltpu.CompilerParams(
-            collective_id=None if solo else 2, has_side_effects=not solo, vmem_limit_bytes=62 * 2**20
-        ),
-        name="forward",
-    )(lengths, inputs, cotangent, *weights, *small)
-
-
-def backward_kernel(
-    splits, copies, solo,
-    lengths_ref, x_row, cot_row, out_row, qx_hbm, kx_hbm, vx_hbm, att_hbm, mid_hbm, nmid_hbm, act_hbm, slope_hbm,
-    narrow_hbm, wqkv_hbm, wo_hbm, w1_hbm, w2_hbm,
-    gain_ref, shift_ref, dm_ref, dh_ref, uq_ref, uh_ref, um_ref,
-    output, dx_out, total_ref,
-    wqkv, wo, w1, w2, kx, vx, dk, dv, x_t, cot_t, mid_t, nmid_t, act_t, slope_t, narrow_t, att_t, qx_t,
-    gx, dq, gmid, dx_s, part, aq, ap, a1, a2, bq, bp, b2, b1,
-    w_sem, t_sem, kv_sem, own_sem, f_sent, f_land, b_sent, b_land,
-    *sum_refs,
-):
-    me = 0 if solo else lax.axis_index("seq")
-    span, width = x_t.shape[1], x_t.shape[2]
-    hidden = w1.shape[1]
-    blocks = TILE // span
-    total = splits * span
-    tiles = total // TILE
-    heads = kx.shape[0]
-    half = LANES // 2
-    length = lengths_ref[me]
-    scale = half ** (-0.5)
-
-    def load_first(tile):
-        rows = pl.ds(tile * TILE, TILE)
-        pairs = (
-            (cot_row.at[pl.ds(tile * blocks, blocks)], cot_t),
-            (slope_hbm.at[rows, :], slope_t),
-            (act_hbm.at[rows, :], act_t),
-            (narrow_hbm.at[rows, :], narrow_t),
-            (mid_hbm.at[rows, :], mid_t),
-            (nmid_hbm.at[rows, :], nmid_t),
-            (att_hbm.at[:, rows, :], att_t),
-        )
-        return [pltpu.make_async_copy(a, b, t_sem.at[i]) for i, (a, b) in enumerate(pairs)]
-
-    def load_q(tile):
-        return pltpu.make_async_copy(qx_hbm.at[:, pl.ds(tile * TILE, TILE), :], qx_t, t_sem.at[7])
-
-    def load_x(tile):
-        return pltpu.make_async_copy(x_row.at[pl.ds(tile * blocks, blocks)], x_t, t_sem.at[8])
-
-    get_w2, get_w1, get_wo, get_wqkv = (
-        pltpu.make_async_copy(source, target, w_sem.at[index])
-        for index, (source, target) in enumerate(((w2_hbm, w2), (w1_hbm, w1), (wo_hbm, wo), (wqkv_hbm, wqkv)))
-    )
-    get_k = pltpu.make_async_copy(kx_hbm, kx, kv_sem.at[0])
-    get_v = pltpu.make_async_copy(vx_hbm, vx, kv_sem.at[1])
-    own_f = pltpu.make_async_copy(out_row.at[me], output.at[me], own_sem.at[0])
-    own_b = pltpu.make_async_copy(dx_s.at[me], dx_out.at[me], own_sem.at[1])
-
-    first = load_first(tiles - 1)
-    first[0].start()
-    get_w2.start()
-    for load in first[1:4]:
-        load.start()
-    get_w1.start()
-    for load in first[4:]:
-        load.start()
-    get_wo.start()
-    load_q(tiles - 1).start()
-    get_k.start()
-    get_v.start()
-    get_wqkv.start()
-    load_x(tiles - 1).start()
-    if not solo:
-        greet((("seq", splits), ("dp", copies)))
-        own_f.start()
-        for slot, peer in enumerate(peer_order(me, splits, True)):
-            send(out_row.at[peer], output.at[me], f_sent.at[slot], f_land.at[me], "seq", peer).start()
-    fill_adapters(dm_ref, dh_ref, uq_ref, uh_ref, um_ref, aq, ap, a1, a2, bq, bp, b2, b1)
-    part[...] = jnp.zeros_like(part)
-
-    lane = lax.broadcasted_iota(jnp.int32, (TILE, LANES), 1)
-    row = lax.broadcasted_iota(jnp.int32, (TILE, TILE), 0)
-    col = lax.broadcasted_iota(jnp.int32, (TILE, TILE), 1)
-    causal = row <= col
-    zero = jnp.zeros((TILE, LANES), jnp.bfloat16)
-    owns = (lane < half, lane >= half)
-    spares = (half, 0)
+        outs[...] = low(result + dotf(narrow_2, b2[...])).reshape(blocks, span, width)
+        narrow[begin:end, RANK : 2 * RANK] = narrow_p
+        narrow[begin:end, 2 * RANK : 3 * RANK] = narrow_1
+        narrow[begin:end, 3 * RANK : 4 * RANK] = narrow_2
+        if tile < tiles - 1:
+            for save in saves(tile):
+                save.start()
+        else:
+            saves(tile)[4].start()
 
     def add_upper(start, value):
         part[0:RANK, start : start + value.shape[1]] += value
@@ -873,24 +792,25 @@
     def add_lower(start, value):
         part[RANK : 2 * RANK, start : start + value.shape[1]] += value
 
-    def b_copy(block):
-        return send(dx_s.at[block], dx_out.at[me], b_sent.at[block], b_land.at[me], "seq", block)
-
+    cot_fetch(tiles - 1)
     for tile in reversed(range(tiles)):
         begin, end = tile * TILE, (tile + 1) * TILE
         newest = tile == tiles - 1
-        for load in load_first(tile):
-            load.wait()
         if newest:
-            get_w2.wait()
-            get_w1.wait()
+            saves(tile)[4].wait()
+            send_output(tile)
+        else:
+            for fetch in fetches(tile)[0:3]:
+                fetch.wait()
+        for block in tile_blocks(tile):
+            cot_move(block, False).wait()
         spot = begin + lax.broadcasted_iota(jnp.int32, (TILE, width), 0)
         given = cot_t[...].reshape(TILE, width)
         gout = jnp.where(spot < length, given, jnp.zeros_like(given))
-        narrow_q = narrow_t[:, 0:RANK]
-        narrow_p = narrow_t[:, RANK : 2 * RANK]
-        narrow_1 = narrow_t[:, 2 * RANK : 3 * RANK]
-        narrow_2 = narrow_t[:, 3 * RANK : 4 * RANK]
+        narrow_q = narrow[begin:end, 0:RANK]
+        narrow_p = narrow[begin:end, RANK : 2 * RANK]
+        narrow_1 = narrow[begin:end, 2 * RANK : 3 * RANK]
+        narrow_2 = narrow[begin:end, 3 * RANK : 4 * RANK]
         gn2 = low(dotf(gout, b2[...], NT))
         add_upper(7 * width, dotf(narrow_2, gout, TN))
         size = 512
@@ -906,49 +826,44 @@
             gact = ahead
             if stop < hidden:
                 ahead = contract(stop)
-            gbefore = low(gact * wide(slope_t[:, start:stop]))
-            add_lower(start, dotf(gn2, act_t[:, start:stop], TN))
+            gbefore = low(gact * wide(slope[:, start:stop]))
+            add_lower(start, dotf(gn2, act[:, start:stop], TN))
             add_lower(hidden + start, dotf(narrow_1, gbefore, TN))
             gn1 = gn1 + dotf(gbefore, b1[:, start:stop], NT)
             gnorm = gnorm + dotf(gbefore, w1[:, start:stop], NT)
         gn1 = low(gn1)
         gnorm = gnorm + dotf(gn1, a1[...])
-        add_upper(2 * width, dotf(gn1, nmid_t[...], TN))
-        unit, scaled = norm_parts(mid_t[...])
+        if not newest:
+            fetches(tile)[3].wait()
+        unit, scaled = norm_parts(mid[...])
+        normed = low(unit * wide(gain_ref[1:2, :]) + wide(shift_ref[1:2, :]))
+        add_upper(2 * width, dotf(gn1, normed, TN))
         grad = wide(gout) + norm_back(gnorm, unit, scaled, wide(gain_ref[1:2, :]))
-        gmid[...] = grad
+        mid[...] = grad
         glow = low(grad)
-        if newest:
-            get_wo.wait()
         gnp = low(dotf(glow, bp[...], NT))
         add_upper(6 * width, dotf(narrow_p, glow, TN))
         gatt = low(dotf(glow, wo[...], NT) + dotf(gnp, ap[...]))
-        attended = jnp.concatenate([att_t[index] for index in range(heads // 2)], axis=1)
+        attended = jnp.concatenate([att[index] for index in range(pairs)], axis=1)
         add_upper(width, dotf(gnp, attended, TN))
-        for index in range(heads // 2):
+        for index in range(pairs):
             piece = gatt[:, index * LANES : (index + 1) * LANES]
-            product = wide(piece) * wide(att_t[index])
+            product = wide(piece) * wide(att[index])
             for parity in range(2):
                 own, spare = owns[parity], spares[parity]
                 delta = -jnp.sum(jnp.where(own, product, 0.0), axis=-1, keepdims=True)
-                high, middle, rest = triple(jnp.broadcast_to(delta, (TILE, LANES)))
-                extra = jnp.where(
-                    lane == spare, high, jnp.where(lane == spare + 1, middle, jnp.where(lane == spare + 2, rest, zero))
-                )
-                gx[2 * index + parity] = jnp.where(own, piece, extra)
+                gx[2 * index + parity] = with_extra(own, spare, piece, jnp.broadcast_to(delta, (TILE, LANES)))
         if tile:
-            for load in load_first(tile - 1):
-                load.start()
-        load_q(tile).wait()
-        if newest:
-            get_k.wait()
-            get_v.wait()
-
-        def attend(index, carry):
+            for fetch in fetches(tile - 1)[0:3]:
+                fetch.start()
+            cot_fetch(tile - 1)
+        causal = row <= col
+
+        def attend_back(index, carry):
             def products(unit):
                 head = index * GROUP + unit
                 return (
-                    dotf(kx[head, 0:end, :], qx_t[head], NT),
+                    dotf(kx[head, 0:end, :], qx[head, begin:end, :], NT),
                     dotf(vx[head, 0:end, :], gx[head], NT),
                 )
 
@@ -960,7 +875,7 @@
                 dscore = low(weights * dprob)
                 return (
                     dotf(dscore, kx[head, 0:end, :], TN),
-                    dotf(dscore, qx_t[head]),
+                    dotf(dscore, qx[head, begin:end, :]),
                     dotf(low(weights), gx[head]),
                 )
 
@@ -986,36 +901,30 @@
                     dv[pair, 0:end, :] += more_v
             return carry
 
-        lax.fori_loop(0, heads // GROUP, attend, 0)
-        if tile:
-            load_q(tile - 1).start()
-        load_x(tile).wait()
-        if newest:
-            get_wqkv.wait()
-        pairs = range(heads // 2)
-        parts = [
-            jnp.concatenate([dq[index] for index in pairs], axis=1),
-            jnp.concatenate([low(dk[index, begin:end, :]) for index in pairs], axis=1),
-            jnp.concatenate([low(dv[index, begin:end, :]) for index in pairs], axis=1),
+        lax.fori_loop(0, heads // GROUP, attend_back, 0)
+        values = [
+            jnp.concatenate([dq[index] for index in range(pairs)], axis=1),
+            jnp.concatenate([low(dk[index, begin:end, :]) for index in range(pairs)], axis=1),
+            jnp.concatenate([low(dv[index, begin:end, :]) for index in range(pairs)], axis=1),
         ]
         gnq = jnp.zeros((TILE, RANK), jnp.float32)
         gnormed = jnp.zeros((TILE, width), jnp.float32)
-        for index, value in enumerate(parts):
+        for index, value in enumerate(values):
             start, stop = index * width, (index + 1) * width
             gnq = gnq + dotf(value, bq[:, start:stop], NT)
             add_upper(3 * width + start, dotf(narrow_q, value, TN))
             gnormed = gnormed + dotf(value, wqkv[:, start:stop], NT)
         gnq = low(gnq)
         gnormed = gnormed + dotf(gnq, aq[...])
-        unit, scaled = norm_parts(wide(x_t[...].reshape(TILE, width)))
+        unit, scaled = norm_parts(wide(xr[tile * blocks : (tile + 1) * blocks].reshape(TILE, width)))
         normed = low(unit * wide(gain_ref[0:1, :]) + wide(shift_ref[0:1, :]))
         add_upper(0, dotf(gnq, normed, TN))
-        dx = low(gmid[...] + norm_back(gnormed, unit, scaled, wide(gain_ref[0:1, :])))
-        dx_s[tile * blocks : (tile + 1) * blocks] = dx.reshape(blocks, span, width)
+        dx = low(mid[...] + norm_back(gnormed, unit, scaled, wide(gain_ref[0:1, :])))
         if tile:
-            load_x(tile - 1).start()
+            fetches(tile - 1)[3].start()
+        xr[tile * blocks : (tile + 1) * blocks] = dx.reshape(blocks, span, width)
         if not solo:
-            for block in range(tile * blocks, (tile + 1) * blocks):
+            for block in tile_blocks(tile):
 
                 @pl.when(me != block)
                 def _():
@@ -1030,73 +939,78 @@
     if solo:
         total_ref[...] = part[...]
         return
+    own_f = pltpu.make_async_copy(out_row.at[me], output.at[me], own_sem.at[2])
+    own_f.start()
     sum_everywhere(splits, copies, part, total_ref, *sum_refs)
     own_f.wait()
     own_b.wait()
-    for slot, peer in enumerate(peer_order(me, splits, True)):
-        send(out_row.at[peer], output.at[peer], f_sent.at[slot], f_land.at[peer], "seq", peer).wait()
-        send(dx_s.at[peer], dx_out.at[peer], b_sent.at[peer], b_land.at[peer], "seq", peer).wait()
-
-
-def backward(splits, copies, solo, lengths, saved, weights, small):
-    span, width = saved[0].shape[1:]
+    for slot, peer in enumerate(far + near):
+        x_copy(peer, slot).wait_send()
+        c_copy(peer, slot).wait_send()
+        send(out_row.at[peer], output.at[peer], f_sent.at[peer], f_land.at[peer], "seq", peer).wait()
+        send(xr.at[peer], dx_out.at[peer], b_sent.at[peer], b_land.at[peer], "seq", peer).wait()
+
+
+def whole_block(splits, copies, solo, lengths, inputs, cotangent, small, weights):
+    span, width = inputs.shape[1:]
+    total = splits * span
     hidden = weights[2].shape[1]
-    total = splits * span
-    heads = saved[3].shape[0]
+    heads = 2 * width // LANES
     blocks = TILE // span
     anyspace = pl.BlockSpec(memory_space=pl.ANY)
     vmem = pl.BlockSpec(memory_space=pltpu.VMEM)
     bf, f32 = jnp.bfloat16, jnp.float32
+    row = (splits, span, width)
+    shapes = [
+        (row, bf),
+        (row, bf),
+        ((2 * RANK, 8 * width), f32),
+        (row, bf),
+        (row, bf),
+        ((heads // 2, total, LANES), bf),
+        ((total, width), f32),
+        ((total, hidden), bf),
+        ((total, hidden), bf),
+    ]
     dma = pltpu.SemaphoreType.DMA
     scratch = [
         *[pltpu.VMEM(w.shape, bf) for w in weights],
         pltpu.VMEM((heads, total, LANES), bf),
         pltpu.VMEM((heads, total, LANES), bf),
+        pltpu.VMEM((heads, total, LANES), bf),
         pltpu.VMEM((heads // 2, total, LANES), f32),
         pltpu.VMEM((heads // 2, total, LANES), f32),
+        pltpu.VMEM(row, bf),
+        pltpu.VMEM((heads // 2, TILE, LANES), bf),
+        pltpu.VMEM((TILE, width), f32),
+        pltpu.VMEM((TILE, hidden), bf),
+        pltpu.VMEM((TILE, hidden), bf),
         pltpu.VMEM((blocks, span, width), bf),
         pltpu.VMEM((blocks, span, width), bf),
-        pltpu.VMEM((TILE, width), f32),
-        pltpu.VMEM((TILE, width), bf),
-        pltpu.VMEM((TILE, hidden), bf),
-        pltpu.VMEM((TILE, hidden), bf),
-        pltpu.VMEM((TILE, LANES), bf),
-        pltpu.VMEM((heads // 2, TILE, LANES), bf),
-        pltpu.VMEM((heads, TILE, LANES), bf),
         pltpu.VMEM((heads, TILE, LANES), bf),
         pltpu.VMEM((heads // 2, TILE, LANES), bf),
-        pltpu.VMEM((TILE, width), f32),
-        pltpu.VMEM((splits, span, width), bf),
+        pltpu.VMEM((total, LANES), bf),
         pltpu.VMEM((2 * RANK, 8 * width), f32),
         *adapter_scratch(width, hidden),
         dma((4,)),
-        dma((9,)),
-        dma((2,)),
-        dma((2,)),
-        dma((splits,)),
-        dma((splits,)),
-        dma((splits,)),
-        dma((splits,)),
+        dma((5,)),
+        dma((4 + blocks,)),
+        dma((3,)),
+        *[dma((splits,)) for _ in range(8)],
     ]
     if not solo:
         scratch += sum_scratch(splits, copies, 8 * width)
     return pl.pallas_call(
-        lambda *refs: backward_kernel(splits, copies, solo, *refs),
-        out_shape=[
-            jax.ShapeDtypeStruct((splits, span, width), bf),
-            jax.ShapeDtypeStruct((splits, span, width), bf),
-            jax.ShapeDtypeStruct((2 * RANK, 8 * width), f32),
-        ],
-        in_specs=[pl.BlockSpec(memory_space=pltpu.SMEM)]
-        + [anyspace] * (len(saved) + len(weights))
-        + [vmem] * len(small),
-        out_specs=[anyspace, anyspace, vmem],
+        lambda *refs: block_kernel(splits, copies, solo, *refs),
+        out_shape=[jax.ShapeDtypeStruct(s, d) for s, d in shapes],
+        in_specs=[pl.BlockSpec(memory_space=pltpu.SMEM)] + [anyspace] * 6 + [vmem] * len(small),
+        out_specs=[anyspace, anyspace, vmem] + [anyspace] * 6,
         scratch_shapes=scratch,
         compiler_params=pltpu.CompilerParams(
-            collective_id=None if solo else 3, has_side_effects=not solo, vmem_limit_bytes=63 * 2**20
+            collective_id=None if solo else 4, has_side_effects=not solo, vmem_limit_bytes=64 * 2**20 - 2**18
         ),
-        name="backward",
-    )(lengths, *saved, *weights, *small)
+        name="block",
+    )(lengths, inputs, cotangent, *weights, *small)[:3]
 
 
 def local_by_heads(
@@ -1300,12 +1214,8 @@
         first_feedforward_weight,
         second_feedforward_weight,
     ]
-    saved = list(forward(
-        pieces, False, lengths, inputs, cotangent, [biases.reshape(1, -1)] + norms + adapters, weights
-    ))
-    saved[2] = saved[2].reshape(inputs.shape)
-    output, input_grad, total = backward(
-        pieces, copies, False, lengths, saved, weights, norms + adapters
+    output, input_grad, total = whole_block(
+        pieces, copies, False, lengths, inputs, cotangent, [biases.reshape(1, -1)] + norms + adapters, weights
     )
     return update(
         total,

time: 279 us -> 248 us (0.89)
  Pallas kernels: 270 us -> 242 us
  local copies, waits for them, and re-layouts: 5.57 us -> 1.35 us
    pallas_call x2 -> x1, Pallas kernels: 267 us -> 236 us  [whole_block(): pl.pallas_call(lambda *refs: block_kernel(splits, copies, solo, *refs), o...]
    unnamed x36 -> x0, local copies, waits for them, and re-layouts: 4.22 us -> none
where the time goes in v3:
time: 248 us; the launch traced here: 244 us
  Pallas kernels  242 us (98%)
    pallas_call x1, Pallas kernels, whole_block(): pl.pallas_call(lambda *refs: block_kernel(splits, copies, solo, *refs), o...  236 us
    pallas_call x1, Pallas kernels, update(): pl.pallas_call(update_kernel, out_shape=[jax.ShapeDtypeStruct(a.shape, a....  5.65 us

profile of v3, /device:TPU:0, one launch (start us, length us, event | category | flops | bytes accessed | tf_op | source)
XLA Modules:
  0.0 244.2 jit_solution(4253594611887609917)
XLA Ops:
  0.7 1.4 reshape.83.refs_7_
  2.0 236.3 %block.1 = (bf16[8,128,1024]{2,1,0:T(8,128)(2,1)}, bf16[8,128,1024]{2,1,0:T(8,128)(2,1)}, f32[8,8192]{1,0:T(8,128)}, bf16[8,128,1024]{2,1,0:T(8,128)(2,1)}, bf16...) custom-call(s32[8]{0:T(128)} %refs_0_.1, ...), custom_call_target="tpu_custom_call" | custom-call | tf_op jit(solution)/shard_map/block/pallas_call | solution.py:1003
  238.3 5.7 %factored_update.1 = (bf16[8,128,1024]{2,1,0:T(8,128)(2,1)}, bf16[8,128,1024]{2,1,0:T(8,128)(2,1)}, f32[3,4,1024]{2,1,0:T(4,128)}, f32[4,4096]{1,0:T(4,128)}, f3...) custom-call(f32[8,8192]{1,0:T(8,128)} %get-tuple-element.47.total_re, ...), custom_call_target="tpu_custom_call" | custom-call | tf_op jit(solution)/shard_map/factored_update/pallas_call | solution.py:427

commit v4 on v3

--- a/solution.py
+++ b/solution.py
@@ -270,66 +270,76 @@
 
 
 def sum_everywhere(
-    splits, copies, part_ref, total_ref, seq_in, dp_in, own, s_sent, s_land, d_sent, d_land, g_sent, g_land
+    splits, copies, part_ref, total_ref, dp_in, seq_in, own, piece, d_sent, d_land, s_sent, s_land, g_sent, g_land, e_sent, e_land
 ):
-    size = part_ref.shape[1] // splits
+    size = part_ref.shape[1] // copies
+    small = size // splits
     me, peers = peers_of("seq", splits)
     mine, others = peers_of("dp", copies)
 
     def columns(index):
         return pl.ds(pl.multiple_of(index * size, size), size)
 
-    first = []
+    def narrow_columns(index, start=0):
+        return pl.ds(pl.multiple_of(start + index * small, small), small)
+
+    sent = []
+
+    def start(copy):
+        copy.start()
+        sent.append(copy)
+
+    for shift, peer in enumerate(others):
+        start(send(part_ref.at[:, columns(peer)], dp_in.at[mine], d_sent.at[shift], d_land.at[mine], "dp", peer))
+    dp_in[mine] = part_ref[:, columns(mine)]
+    for peer in others:
+        send(part_ref.at[:, columns(mine)], dp_in.at[peer], d_sent.at[0], d_land.at[peer], "dp", peer).wait_recv()
+    summed = dp_in[0]
+    for index in range(1, copies):
+        summed = summed + dp_in[index]
+    own[...] = summed
     for shift, peer in enumerate(peers):
-        copy = send(part_ref.at[:, columns(peer)], seq_in.at[me], s_sent.at[shift], s_land.at[me], "seq", peer)
-        copy.start()
-        first.append(copy)
-    seq_in[me] = part_ref[:, columns(me)]
+        start(send(own.at[:, narrow_columns(peer)], seq_in.at[me], s_sent.at[shift], s_land.at[me], "seq", peer))
+    seq_in[me] = own[:, narrow_columns(me)]
     for peer in peers:
-        send(part_ref.at[:, columns(me)], seq_in.at[peer], s_sent.at[0], s_land.at[peer], "seq", peer).wait_recv()
+        send(own.at[:, narrow_columns(me)], seq_in.at[peer], s_sent.at[0], s_land.at[peer], "seq", peer).wait_recv()
     summed = seq_in[0]
     for index in range(1, splits):
         summed = summed + seq_in[index]
-    own[...] = summed
-    second = []
+    piece[...] = summed
+    base = mine * size
+    total_ref[:, narrow_columns(me, base)] = summed
+    for shift, peer in enumerate(peers):
+        start(send(piece, total_ref.at[:, narrow_columns(me, base)], g_sent.at[shift], g_land.at[me], "seq", peer))
+    for peer in peers:
+        send(piece, total_ref.at[:, narrow_columns(peer, base)], g_sent.at[0], g_land.at[peer], "seq", peer).wait_recv()
     for shift, peer in enumerate(others):
-        copy = send(own, dp_in.at[mine], d_sent.at[shift], d_land.at[mine], "dp", peer)
-        copy.start()
-        second.append(copy)
-    dp_in[mine] = summed
+        part = total_ref.at[:, columns(mine)]
+        start(send(part, part, e_sent.at[shift], e_land.at[mine], "dp", peer))
     for peer in others:
-        send(own, dp_in.at[peer], d_sent.at[0], d_land.at[peer], "dp", peer).wait_recv()
-    summed = dp_in[0]
-    for index in range(1, copies):
-        summed = summed + dp_in[index]
-    total_ref[:, columns(me)] = summed
-    third = []
-    for shift, peer in enumerate(peers):
-        copy = send(
-            total_ref.at[:, columns(me)], total_ref.at[:, columns(me)], g_sent.at[shift], g_land.at[me], "seq", peer
-        )
-        copy.start()
-        third.append(copy)
-    for peer in peers:
         part = total_ref.at[:, columns(peer)]
-        send(part, part, g_sent.at[0], g_land.at[peer], "seq", peer).wait_recv()
-    for copy in first + second + third:
+        send(part, part, e_sent.at[0], e_land.at[peer], "dp", peer).wait_recv()
+    for copy in sent:
         copy.wait_send()
 
 
 def sum_scratch(splits, copies, width):
-    size = width // splits
+    size = width // copies
+    small = size // splits
     dma = pltpu.SemaphoreType.DMA
     return [
-        pltpu.VMEM((splits, 8, size), jnp.float32),
         pltpu.VMEM((copies, 8, size), jnp.float32),
+        pltpu.VMEM((splits, 8, small), jnp.float32),
         pltpu.VMEM((8, size), jnp.float32),
+        pltpu.VMEM((8, small), jnp.float32),
+        dma((copies,)),
+        dma((copies,)),
+        dma((splits,)),
+        dma((splits,)),
         dma((splits,)),
         dma((splits,)),
         dma((copies,)),
         dma((copies,)),
-        dma((splits,)),
-        dma((splits,)),
     ]
 
 
@@ -501,6 +511,8 @@
     own_x = pltpu.make_async_copy(inputs if solo else inputs.at[me], xr if solo else xr.at[me], own_sem.at[0])
     own_b = pltpu.make_async_copy(xr.at[me], dx_out.at[me], own_sem.at[1])
 
+    own_f = pltpu.make_async_copy(out_row.at[me], output.at[me], own_sem.at[2])
+
     def saves(tile):
         rows = pl.ds(tile * TILE, TILE)
         moves = (
@@ -582,19 +594,19 @@
     loads[0].start()
     if not solo:
         far, near = peer_order(me, splits)
-        quarter = lax.rem(me, splits // 2) // 2
-        outward = jnp.logical_or(
-            jnp.logical_and(me < splits // 2, quarter == 0), jnp.logical_and(upper, quarter == 0)
-        )
-
-        @pl.when(outward)
+        early = lax.rem(me, splits // 2) < splits // 4
+        lower_early = jnp.logical_and(early, jnp.logical_not(upper))
+        lower_late = jnp.logical_and(jnp.logical_not(early), jnp.logical_not(upper))
+        ways = list(enumerate(far + near))
+
+        @pl.when(jnp.logical_not(lower_early))
         def _():
-            for slot, peer in enumerate(far + near):
+            for slot, peer in ways[len(far) :]:
                 x_copy(peer, slot).start()
 
-        @pl.when(jnp.logical_not(outward))
+        @pl.when(jnp.logical_not(lower_late))
         def _():
-            for slot, peer in enumerate(near + far):
+            for slot, peer in ways[: len(far)]:
                 x_copy(peer, slot).start()
 
     for load in loads[1:]:
@@ -610,6 +622,20 @@
     scale = half ** (-0.5)
     owns = (lane < half, lane >= half)
     spares = (half, 0)
+
+    def absorb(weight, down, up):
+        rows, columns = weight.shape
+        size = 1024
+
+        def step(index, carry):
+            span_rows = pl.ds(pl.multiple_of(index * TILE, TILE), TILE)
+            left = down[:, span_rows]
+            for start in range(0, columns, size):
+                part_ref = weight.at[span_rows, pl.ds(start, size)]
+                part_ref[...] = low(wide(part_ref[...]) + dotf(left, up[:, start : start + size], TN))
+            return carry
+
+        lax.fori_loop(0, rows // TILE, step, 0)
 
     def with_extra(own, spare, value, extra):
         high, middle, rest = triple(extra)
@@ -640,7 +666,7 @@
         for index in range(3):
             for start in range(0, width, size):
                 column = index * width + start
-                value = dotf(normed, wqkv[:, column : column + size]) + dotf(narrow_q, bq[:, column : column + size])
+                value = dotf(normed, wqkv[:, column : column + size])
                 if index == 0:
                     value = value + bias(start, size)
                 if index == 2:
@@ -660,19 +686,35 @@
                         else:
                             vx[head, rows, :] = jnp.where(own, piece, one)
 
+    own_x.wait()
+    loads[0].wait()
+    absorb(wqkv, aq, bq)
+    loads[1].wait()
+    absorb(wo, ap, bp)
+    if not solo:
+
+        @pl.when(lower_early)
+        def _():
+            for slot, peer in ways[len(far) :]:
+                x_copy(peer, slot).start()
+
+    loads[2].wait()
+    absorb(w1, a1, b1)
+    if not solo:
+
+        @pl.when(lower_late)
+        def _():
+            for slot, peer in ways[: len(far)]:
+                x_copy(peer, slot).start()
+
+    loads[3].wait()
+    absorb(w2, a2, b2)
     if not solo:
 
         @pl.when(upper)
         def _():
             for tile in range(tiles // 2, tiles):
                 x_wait(tile)
-
-    own_x.wait()
-    loads[0].wait()
-    if not solo:
-
-        @pl.when(upper)
-        def _():
             lax.fori_loop(tiles // 2, tiles, lambda tile, carry: (project(tile), carry)[1], 0)
 
     for tile in range(tiles):
@@ -690,7 +732,8 @@
                 project(tile)
 
         if not solo:
-            ready = upper if tile == tiles // 2 - 1 else jnp.logical_not(upper)
+            last_tile = jnp.logical_and(upper, jnp.logical_not(early))
+            ready = last_tile if tile == tiles // 2 - 1 else jnp.logical_not(last_tile)
             if tile == tiles // 2 - 1 or tile == tiles // 2:
 
                 @pl.when(ready)
@@ -733,20 +776,15 @@
             return carry
 
         lax.fori_loop(0, heads // GROUP, attend, 0)
-        if tile == 0:
-            for load in loads[1:]:
-                load.wait()
-        else:
+        if tile:
             for save in saves(tile - 1)[1:]:
                 save.wait()
-            send_output(tile - 1)
         attended = jnp.concatenate([att[index] for index in range(pairs)], axis=1)
         narrow_p = low(dotf(attended, ap[...], NT))
         middle = (
             wide(xr[tile * blocks : (tile + 1) * blocks].reshape(TILE, width))
             + dotf(attended, wo[...])
             + bias(2 * width, width)
-            + dotf(narrow_p, bp[...])
         )
         mid[...] = middle
         unit, _ = norm_parts(middle)
@@ -755,11 +793,7 @@
         size = 256
 
         def expand(start):
-            return (
-                dotf(normed, w1[:, start : start + size])
-                + bias(3 * width + start, size)
-                + dotf(narrow_1, b1[:, start : start + size])
-            )
+            return dotf(normed, w1[:, start : start + size]) + bias(3 * width + start, size)
 
         result = middle + bias(3 * width + hidden, width)
         narrow_2 = jnp.zeros((TILE, RANK), jnp.float32)
@@ -776,7 +810,7 @@
             result = result + dotf(active, w2[start:stop, :])
             narrow_2 = narrow_2 + dotf(active, a2[:, start:stop], NT)
         narrow_2 = low(narrow_2)
-        outs[...] = low(result + dotf(narrow_2, b2[...])).reshape(blocks, span, width)
+        outs[...] = low(result).reshape(blocks, span, width)
         narrow[begin:end, RANK : 2 * RANK] = narrow_p
         narrow[begin:end, 2 * RANK : 3 * RANK] = narrow_1
         narrow[begin:end, 3 * RANK : 4 * RANK] = narrow_2
@@ -797,8 +831,7 @@
         begin, end = tile * TILE, (tile + 1) * TILE
         newest = tile == tiles - 1
         if newest:
-            saves(tile)[4].wait()
-            send_output(tile)
+            pass
         else:
             for fetch in fetches(tile)[0:3]:
                 fetch.wait()
@@ -816,7 +849,7 @@
         size = 512
 
         def contract(start):
-            return dotf(gout, w2[start : start + size, :], NT) + dotf(gn2, a2[:, start : start + size])
+            return dotf(gout, w2[start : start + size, :], NT)
 
         gnorm = jnp.zeros((TILE, width), jnp.float32)
         gn1 = jnp.zeros((TILE, RANK), jnp.float32)
@@ -832,7 +865,6 @@
             gn1 = gn1 + dotf(gbefore, b1[:, start:stop], NT)
             gnorm = gnorm + dotf(gbefore, w1[:, start:stop], NT)
         gn1 = low(gn1)
-        gnorm = gnorm + dotf(gn1, a1[...])
         if not newest:
             fetches(tile)[3].wait()
         unit, scaled = norm_parts(mid[...])
@@ -843,7 +875,7 @@
         glow = low(grad)
         gnp = low(dotf(glow, bp[...], NT))
         add_upper(6 * width, dotf(narrow_p, glow, TN))
-        gatt = low(dotf(glow, wo[...], NT) + dotf(gnp, ap[...]))
+        gatt = low(dotf(glow, wo[...], NT))
         attended = jnp.concatenate([att[index] for index in range(pairs)], axis=1)
         add_upper(width, dotf(gnp, attended, TN))
         for index in range(pairs):
@@ -857,6 +889,12 @@
             for fetch in fetches(tile - 1)[0:3]:
                 fetch.start()
             cot_fetch(tile - 1)
+        if newest:
+            saves(tile)[4].wait()
+            for done in range(tiles):
+                send_output(done)
+            if not solo:
+                own_f.start()
         causal = row <= col
 
         def attend_back(index, carry):
@@ -915,7 +953,6 @@
             add_upper(3 * width + start, dotf(narrow_q, value, TN))
             gnormed = gnormed + dotf(value, wqkv[:, start:stop], NT)
         gnq = low(gnq)
-        gnormed = gnormed + dotf(gnq, aq[...])
         unit, scaled = norm_parts(wide(xr[tile * blocks : (tile + 1) * blocks].reshape(TILE, width)))
         normed = low(unit * wide(gain_ref[0:1, :]) + wide(shift_ref[0:1, :]))
         add_upper(0, dotf(gnq, normed, TN))
@@ -939,8 +976,6 @@
     if solo:
         total_ref[...] = part[...]
         return
-    own_f = pltpu.make_async_copy(out_row.at[me], output.at[me], own_sem.at[2])
-    own_f.start()
     sum_everywhere(splits, copies, part, total_ref, *sum_refs)
     own_f.wait()
     own_b.wait()

time: 248 us -> 229 us (0.923)
  Pallas kernels: 242 us -> 223 us
    pallas_call x1, Pallas kernels: 236 us -> 218 us  [whole_block(): pl.pallas_call(lambda *refs: block_kernel(splits, copies, solo, *refs), o...]
where the time goes in v4:
time: 229 us; the launch traced here: 226 us
  Pallas kernels  223 us (97%)
    pallas_call x1, Pallas kernels, whole_block(): pl.pallas_call(lambda *refs: block_kernel(splits, copies, solo, *refs), o...  218 us
    pallas_call x1, Pallas kernels, update(): pl.pallas_call(update_kernel, out_shape=[jax.ShapeDtypeStruct(a.shape, a....  5.65 us

profile of v4, /device:TPU:0, one launch (start us, length us, event | category | flops | bytes accessed | tf_op | source)
XLA Modules:
  0.0 225.7 jit_solution(15059655761883444885)
XLA Ops:
  0.7 1.4 reshape.83.refs_7_
  2.0 217.7 %block.1 = (bf16[8,128,1024]{2,1,0:T(8,128)(2,1)}, bf16[8,128,1024]{2,1,0:T(8,128)(2,1)}, f32[8,8192]{1,0:T(8,128)}, bf16[8,128,1024]{2,1,0:T(8,128)(2,1)}, bf16...) custom-call(s32[8]{0:T(128)} %refs_0_.1, ...), custom_call_target="tpu_custom_call" | custom-call | tf_op jit(solution)/shard_map/block/pallas_call | solution.py:1038
  219.8 5.7 %factored_update.1 = (bf16[8,128,1024]{2,1,0:T(8,128)(2,1)}, bf16[8,128,1024]{2,1,0:T(8,128)(2,1)}, f32[3,4,1024]{2,1,0:T(4,128)}, f32[4,4096]{1,0:T(4,128)}, f3...) custom-call(f32[8,8192]{1,0:T(8,128)} %get-tuple-element.47.total_re, ...), custom_call_target="tpu_custom_call" | custom-call | tf_op jit(solution)/shard_map/factored_update/pallas_call | solution.py:437

commit v5 on v4

--- a/solution.py
+++ b/solution.py
@@ -385,16 +385,19 @@
     output_out, grad_out, g_dm, g_dh, g_uq, g_uh, g_um, n_dm, n_dh, n_uq, n_uh, n_um,
     r_dm, r_dh, r_uq, r_uh, r_um, c_dm, c_dh, c_uq, c_uh, c_um, held_out, held_grad, sems,
 ):
-    moves = [
-        pltpu.make_async_copy(output_in, held_out, sems.at[0]),
-        pltpu.make_async_copy(grad_in, held_grad, sems.at[1]),
-    ]
-    for move in moves:
+    moves = []
+    for index in range(output_in.shape[0]):
+        for place, (source, held, target) in enumerate(
+            ((output_in, held_out, output_out), (grad_in, held_grad, grad_out))
+        ):
+            moves.append(
+                (
+                    pltpu.make_async_copy(source.at[index], held.at[index], sems.at[place, index]),
+                    pltpu.make_async_copy(held.at[index], target.at[index], sems.at[place, index]),
+                )
+            )
+    for move, _ in moves:
         move.start()
-    moves = [
-        (moves[0], pltpu.make_async_copy(held_out, output_out, sems.at[0])),
-        (moves[1], pltpu.make_async_copy(held_grad, grad_out, sems.at[1])),
-    ]
     for move, onward in moves:
         move.wait()
         onward.start()
@@ -442,7 +445,7 @@
         scratch_shapes=[
             pltpu.VMEM(output.shape, output.dtype),
             pltpu.VMEM(output.shape, output.dtype),
-            pltpu.SemaphoreType.DMA((2,)),
+            pltpu.SemaphoreType.DMA((2, output.shape[0])),
         ],
         compiler_params=pltpu.CompilerParams(vmem_limit_bytes=60 * 2**20),
         name="factored_update",
@@ -488,7 +491,7 @@
     bias_ref, gain_ref, shift_ref, dm_ref, dh_ref, uq_ref, uh_ref, um_ref,
     output, dx_out, total_ref, cot_in, out_row, att_hbm, mid_hbm, act_hbm, slope_hbm,
     wqkv, wo, w1, w2, kx, vx, qx, dk, dv, xr, att, mid, act, slope, cot_t, outs, gx, dq, narrow, part,
-    aq, ap, a1, a2, bq, bp, b2, b1,
+    bias_row, aq, ap, a1, a2, bq, bp, b2, b1,
     w_sem, s_sem, l_sem, own_sem, x_sent, x_land, c_sent, c_land, f_sent, f_land, b_sent, b_land,
     *sum_refs,
 ):
@@ -613,6 +616,9 @@
         load.start()
     fill_adapters(dm_ref, dh_ref, uq_ref, uh_ref, um_ref, aq, ap, a1, a2, bq, bp, b2, b1)
     part[...] = jnp.zeros_like(part)
+    bias_lines = wide(bias_ref[...])
+    for index in range(bias_ref.shape[0]):
+        bias_row[0:1, index * LANES : (index + 1) * LANES] = bias_lines[index : index + 1, :]
 
     lane = lax.broadcasted_iota(jnp.int32, (TILE, LANES), 1)
     row = lax.broadcasted_iota(jnp.int32, (TILE, TILE), 0)
@@ -646,7 +652,7 @@
         )
 
     def bias(start, size):
-        return wide(bias_ref[0:1, start : start + size])
+        return bias_row[0:1, start : start + size]
 
     def rows_of(tile):
         if isinstance(tile, int):
@@ -1026,6 +1032,7 @@
         pltpu.VMEM((heads // 2, TILE, LANES), bf),
         pltpu.VMEM((total, LANES), bf),
         pltpu.VMEM((2 * RANK, 8 * width), f32),
+        pltpu.VMEM((1, small[0].size), f32),
         *adapter_scratch(width, hidden),
         dma((4,)),
         dma((5,)),
@@ -1250,7 +1257,7 @@
         second_feedforward_weight,
     ]
     output, input_grad, total = whole_block(
-        pieces, copies, False, lengths, inputs, cotangent, [biases.reshape(1, -1)] + norms + adapters, weights
+        pieces, copies, False, lengths, inputs, cotangent, [biases.reshape(-1, LANES)] + norms + adapters, weights
     )
     return update(
         total,

time: 229 us -> 228 us (level)
  no operation moved by 1% of the time
where the time goes in v5:
time: 228 us; the launch traced here: 225 us
  Pallas kernels  224 us (98%)
    pallas_call x1, Pallas kernels, whole_block(): pl.pallas_call(lambda *refs: block_kernel(splits, copies, solo, *refs), o...  218 us
    pallas_call x1, Pallas kernels, update(): pl.pallas_call(update_kernel, out_shape=[jax.ShapeDtypeStruct(a.shape, a....  5.76 us

profile of v5, /device:TPU:0, one launch (start us, length us, event | category | flops | bytes accessed | tf_op | source)
XLA Modules:
  0.0 224.5 jit_solution(2064419600271662057)
XLA Ops:
  0.7 217.9 %block.1 = (bf16[8,128,1024]{2,1,0:T(8,128)(2,1)}, bf16[8,128,1024]{2,1,0:T(8,128)(2,1)}, f32[8,8192]{1,0:T(8,128)}, bf16[8,128,1024]{2,1,0:T(8,128)(2,1)}, bf16...) custom-call(s32[8]{0:T(128)} %refs_0_.1, ...), custom_call_target="tpu_custom_call" | custom-call | tf_op jit(solution)/shard_map/block/pallas_call | solution.py:1045
  218.5 5.8 %factored_update.1 = (bf16[8,128,1024]{2,1,0:T(8,128)(2,1)}, bf16[8,128,1024]{2,1,0:T(8,128)(2,1)}, f32[3,4,1024]{2,1,0:T(4,128)}, f32[4,4096]{1,0:T(4,128)}, f3...) custom-call(f32[8,8192]{1,0:T(8,128)} %get-tuple-element.47.total_re, ...), custom_call_target="tpu_custom_call" | custom-call | tf_op jit(solution)/shard_map/factored_update/pallas_call | solution.py:440
